TPU v7x, 512 devices: a whole 4x8x8 slice. The times are simulated.
512 devices in a mesh: row: 32 (over y, x), col: 16 (over z, core).
Axes of the slice: x: 4, y: 8, z: 8, core: 2. Of those that a mesh axis runs over, the one named last changes fastest.
Arguments:
- panel: float32 [2, 8192, 256], P(None, 'row', 'col'), may hold values from -100 to 100
- matrix: float32 [2, 8192, 4, 4096], P(None, 'row', None, 'col'), may hold values from -85 to 85
Outputs:
- updated: float32 [2, 8192, 4, 4096], P(None, 'row', None, 'col')
- r_factor: float32 [256, 256], replicated
All inputs are finite; a program needn't handle non-finite values.
Results may differ from a plain program's by a relative error of at most 0.000092.
Values sent between devices are 32-bit elements; how exact they have to be, the bound alone decides.
A program may use at most 64 MiB of HBM per device.

v0:
```python
import jax
import jax.numpy as jnp
from jax import lax
from jax.sharding import PartitionSpec as P

precise = lax.Precision.HIGHEST


def from_root(block, axis, source):
    block = jnp.where(lax.axis_index(axis) == source, block, jnp.zeros_like(block))
    return lax.psum(block, axis)


def matmul(left, right):
    return jnp.dot(left, right, preferred_element_type=jnp.float32, precision=precise)


def inner_left(left, right):
    return lax.dot_general(
        left, right, (((0,), (0,)), ((), ())), preferred_element_type=jnp.float32, precision=precise
    )


def inner_right(left, right):
    return lax.dot_general(
        left, right, (((1,), (1,)), ((), ())), preferred_element_type=jnp.float32, precision=precise
    )


def right_solve(lower, values):
    return lax.linalg.triangular_solve(lower, values, left_side=False, lower=True, transpose_a=True)


def invert(square):
    normal = matmul(square.T, square)
    factor = jnp.linalg.cholesky(normal)
    middle = lax.linalg.triangular_solve(factor, square.T, left_side=True, lower=True)
    return lax.linalg.triangular_solve(factor, middle, left_side=True, lower=True, transpose_a=True)


def alternate(copies, cyc_rows):
    breadth = copies[0].shape[1]
    stacked = jnp.stack([copied.reshape(cyc_rows, -1, breadth) for copied in copies], axis=1)
    return stacked.reshape(-1, breadth)


def per_device(panel, matrix):
    cyc_rows, breadth, cyc_cols, _ = matrix.shape
    row_count = lax.axis_size("row")
    col_count = lax.axis_size("col")
    ratio = row_count // col_count
    row_index = lax.axis_index("row")
    col_index = lax.axis_index("col")
    square = matrix.reshape(cyc_rows * breadth, cyc_cols * breadth)
    slab = lax.all_gather(panel, "col", axis=2, tiled=True).reshape(cyc_rows * breadth, breadth)
    lower_one = jnp.linalg.cholesky(lax.psum(inner_left(slab, slab), "row"))
    basis = right_solve(lower_one, slab)
    r_factor = lower_one.T
    leading = from_root(basis[:breadth], "row", 0)
    identity = jnp.eye(breadth, dtype=jnp.float32)
    transform = invert(identity + leading.T)
    on_top = (row_index == 0).astype(jnp.float32)
    vectors = basis.at[:breadth].add(identity * on_top)
    spread = [from_root(vectors, "row", offset * col_count + col_index) for offset in range(ratio)]
    vectors_cols = alternate(spread, cyc_rows)
    product_rows = lax.psum(matmul(square, vectors_cols), "col")
    scaled_rows = matmul(product_rows, transform)
    coupling = matmul(transform.T, lax.psum(inner_left(vectors, scaled_rows), "row"))
    update_rows = scaled_rows - 0.5 * matmul(vectors, coupling)
    copies = [
        from_root(update_rows, "row", offset * col_count + col_index) for offset in range(ratio)
    ]
    update_cols = alternate(copies, cyc_rows)
    updated = square - inner_right(update_rows, vectors_cols) - inner_right(vectors, update_cols)
    return (updated.reshape(matrix.shape), r_factor)


def solution(mesh):
    in_specs = (P(None, "row", "col"), P(None, "row", None, "col"))
    out_specs = (P(None, "row", None, "col"), P())
    return jax.shard_map(
        per_device, mesh=mesh, in_specs=in_specs, out_specs=out_specs, check_vma=False
    )
```

profile of v0, /device:TPU:1, one launch (start us, length us, event | category | flops | bytes accessed | tf_op | source)
XLA Modules:
  0.0 937.6 jit_solution(4216227946660991040)
XLA Ops:
  7.2 26.2 %all_gather.3 = f32[2,256,256]{1,2,0:T(8,128)S(1)} all-gather(f32[2,256,16]{1,2,0:T(8,128)} %param.5), channel_id=1, replica_groups=mesh['row'=32,'col'=16] {'col'}, dimensions={2}, use_global_device_ids=true | all-gather | bytes 557056 | tf_op jit(solution)/shard_map/all_gather | solution.py:55
  35.0 147.0 %all-reduce.9.cloned.1.call-done = f32[256,256]{0,1:T(8,128)} async-done(((f32[256,256]{0,1:T(8,128)}), f32[256,256]{0,1:T(8,128)}) %all-reduce.9.cloned.1.call-update) | async-done | bytes 262160 | tf_op jit(solution)/shard_map/psum | solution.py:56
  184.1 11.7 %cholesky.130 = f32[128,128]{1,0:T(8,128)S(1)} custom-call(f32[128,128]{1,0:T(8,128)S(1)} %cholesky.194), custom_call_target="Cholesky" | custom-call | tf_op jit(solution)/shard_map/jit(cholesky)/cholesky | solution.py:56
  195.9 9.8 %custom-call.19 = f32[1,128,128]{1,2,0:T(8,128)S(1)} custom-call(f32[1,128,128]{2,1,0:T(8,128)S(1)} %get-tuple-element.75), custom_call_target="InvertDiagBlocksLowerTriangular" | custom-call | tf_op jit(solution)/shard_map/jit(cholesky)/cholesky | solution.py:56
  206.2 11.7 %cholesky.147 = f32[128,128]{1,0:T(8,128)S(1)} custom-call(f32[128,128]{1,0:T(8,128)S(1)} %convolution_subtract_fusion.4), custom_call_target="Cholesky" | custom-call | tf_op jit(solution)/shard_map/jit(cholesky)/cholesky | solution.py:56
  220.8 4.3 while.3
  221.7 1.3 bitcast_dynamic-update-slice_fusion.4
  223.8 1.3 bitcast_dynamic-update-slice_fusion.4
  225.1 19.7 %custom-call.16 = f32[2,128,128]{1,2,0:T(8,128)S(1)} custom-call(f32[2,128,128]{2,1,0:T(8,128)S(1)} %get-tuple-element.22), custom_call_target="InvertDiagBlocksLowerTriangular" | custom-call | tf_op jit(solution)/shard_map/triangular_solve | solution.py:31
  249.5 2.1 copy.38
  251.5 157.7 %all-reduce.17.cloned.1.call-done = (f32[2,1,256,256]{3,2,1,0:T(8,128)}, f32[2,1,256,256]{3,2,1,0:T(8,128)}, f32[256,256]{1,0:T(8,128)}) async-done(((f32[2,1,256,256]{3,2,1,0:T(8,128)}, f32[2,1,256,256]{3,2,1,0:T(8,128)}, f32[256,256]{1,0:T(8,128)}), (f32[2,1,256,256]{3,2,1,0:T(8,128)}, f32[2,1,256,256]{3,2,1,0:T(8,128)}, f32[256,256]{1,0:T(8,128)})) %all-reduce.17.cloned.1.call-update) | async-done | bytes 1310736 | tf_op jit(solution)/shard_map/psum | solution.py:11
  410.2 1.4 fusion.5
  412.5 11.7 %cholesky.164 = f32[128,128]{1,0:T(8,128)S(1)} custom-call(f32[128,128]{1,0:T(8,128)S(1)} %cholesky.197), custom_call_target="Cholesky" | custom-call | tf_op jit(solution)/shard_map/jit(cholesky)/cholesky | solution.py:36
  425.0 9.8 %custom-call.20 = f32[1,128,128]{1,2,0:T(8,128)S(1)} custom-call(f32[1,128,128]{2,1,0:T(8,128)S(1)} %get-tuple-element.71), custom_call_target="InvertDiagBlocksLowerTriangular" | custom-call | tf_op jit(solution)/shard_map/jit(cholesky)/cholesky | solution.py:36
  437.0 11.7 %cholesky.181 = f32[128,128]{1,0:T(8,128)S(1)} custom-call(f32[128,128]{1,0:T(8,128)S(1)} %convolution_subtract_fusion.3), custom_call_target="Cholesky" | custom-call | tf_op jit(solution)/shard_map/jit(cholesky)/cholesky | solution.py:36
  450.8 4.5 while.4
  451.8 1.4 bitcast_dynamic-update-slice_fusion.5
  453.8 1.4 bitcast_dynamic-update-slice_fusion.5
  455.3 19.7 %custom-call.17 = f32[2,128,128]{1,2,0:T(8,128)S(1)} custom-call(f32[2,128,128]{2,1,0:T(8,128)S(1)} %get-tuple-element.30), custom_call_target="InvertDiagBlocksLowerTriangular" | custom-call | tf_op jit(solution)/shard_map/triangular_solve | solution.py:38
  478.4 4.5 convolution_bitcast_fusion
  483.5 117.1 %all-reduce.11.cloned.1.call-done = f32[512,256]{0,1:T(8,128)} async-done(((f32[512,256]{0,1:T(8,128)}), f32[512,256]{0,1:T(8,128)}) %all-reduce.11.cloned.1.call-update) | async-done | bytes 524304 | tf_op jit(solution)/shard_map/psum | solution.py:66
  600.6 2.0 fusion.11
  605.2 149.5 %all-reduce.13.cloned.1.call-done = f32[256,256]{1,0:T(8,128)} async-done(((f32[256,256]{1,0:T(8,128)}), f32[256,256]{1,0:T(8,128)}) %all-reduce.13.cloned.1.call-update) | async-done | bytes 262160 | tf_op jit(solution)/shard_map/psum | solution.py:68
  754.6 1.5 fusion.10
  756.2 2.7 broadcast_select_fusion.1
  758.9 2.1 copy.30
  761.0 2.1 copy.31
  764.0 6.0 fusion.33
  770.0 150.9 %all-reduce.15.cloned.1.call-done = (f32[2,1,256,256]{3,2,1,0:T(8,128)}, f32[2,1,256,256]{3,2,1,0:T(8,128)}) async-done(((f32[2,1,256,256]{3,2,1,0:T(8,128)}, f32[2,1,256,256]{3,2,1,0:T(8,128)}), (f32[2,1,256,256]{3,2,1,0:T(8,128)}, f32[2,1,256,256]{3,2,1,0:T(8,128)})) %all-reduce.15.cloned.1.call-update) | async-done | bytes 1048592 | tf_op jit(solution)/shard_map/psum | solution.py:11
  920.9 1.4 pad_maximum_fusion.1
  922.8 4.9 subtract_subtract_fusion
  927.7 3.2 reshape.72
  (74 shorter events, 26.3 us)
Async XLA Ops:
  7.2 174.9 %all-reduce.9.cloned.1.call-start = ((), (), s32[]{:S(2)}) async-start(), calls=%async_computation | async-start | bytes 524288 | tf_op jit(solution)/shard_map/psum | solution.py:56
  34.7 374.5 %all-reduce.17.cloned.1.call-start = ((), (), s32[]{:S(2)}) async-start(), calls=%async_computation.4 | async-start | bytes 2621440 | tf_op jit(solution)/shard_map/psum | solution.py:11
  249.4 351.2 %all-reduce.11.cloned.1.call-start = ((), (), s32[]{:S(2)}) async-start(), calls=%async_computation.1 | async-start | bytes 1048576 | tf_op jit(solution)/shard_map/psum | solution.py:66
  411.8 0.7 copy-start.3
  477.4 1.0 copy-start
  482.9 271.8 %all-reduce.13.cloned.1.call-start = ((), (), s32[]{:S(2)}) async-start(), calls=%async_computation.2 | async-start | bytes 524288 | tf_op jit(solution)/shard_map/psum | solution.py:68
  604.0 316.9 %all-reduce.15.cloned.1.call-start = ((), (), s32[]{:S(2)}) async-start(), calls=%async_computation.3 | async-start | bytes 2097152 | tf_op jit(solution)/shard_map/psum | solution.py:11
  758.9 4.2 copy-start.2
  920.9 1.9 copy-start.1
Sparse Core Ops, SparseCore 0:
  34.9 147.1 all-reduce.8
  249.5 159.6 all-reduce.16
  483.0 117.5 all-reduce.10
  604.1 150.5 all-reduce.12
  763.2 157.6 all-reduce.14
where the time goes:
time: 955 us; the launch traced here: 938 us
  waiting for transfers between devices  722 us (76%)
  other arithmetic  114 us (12%)
  matrix products  31.5 us (3%)
  blocking collectives  26.2 us (3%)
  local copies, waits for them, and re-layouts  25.1 us (3%)
  between operations  17 us (2%)
    psum x2, waiting for transfers between devices, from_root(): return lax.psum(block, axis)  309 us
    psum x1, waiting for transfers between devices, per_device(): lax.psum(inner_left(vectors, scaled_rows), 'row')  149 us
    psum x1, waiting for transfers between devices, per_device(): lower_one = jnp.linalg.cholesky(lax.psum(inner_left(slab, slab), 'row'))  147 us
    psum x1, waiting for transfers between devices, per_device(): product_rows = lax.psum(matmul(square, vectors_cols), 'col')  117 us
    another operation x7, other arithmetic, invert(): factor = jnp.linalg.cholesky(normal)  34.7 us
    another operation x6, other arithmetic, per_device(): lower_one = jnp.linalg.cholesky(lax.psum(inner_left(slab, slab), 'row'))  34 us
    all_gather x1, blocking collectives, per_device(): lax.all_gather(panel, 'col', axis=2, tiled=True)  26.2 us
    another operation x3, other arithmetic, right_solve(): lax.linalg.triangular_solve(lower, values, left_side=False, lower=True, t...  19.7 us
  transfers between devices with their start and end apart: 5, of which 5 were waited for; matrix products, arithmetic and copies ran while one was open for 1% of the time, Pallas kernels for 0%

commit v1 on v0

v1 whole, which is shorter than its diff:
```python
import functools

import jax
import jax.numpy as jnp
from jax import lax
from jax.experimental import pallas as pl
from jax.experimental.pallas import tpu as pltpu
from jax.sharding import PartitionSpec as P

MESH = pl.DeviceIdType.MESH
precise = lax.Precision.HIGHEST
NX, NY, NZ = 4, 8, 8
NB = 256
PIECE = 16
SLICE = 32
VMEM_LIMIT = 40 * 1024 * 1024


def dot(left, right, contract=((1,), (0,))):
    return lax.dot_general(
        left, right, (contract, ((), ())), preferred_element_type=jnp.float32, precision=precise
    )


def remote(src, dst, send, recv, device):
    return pltpu.make_async_remote_copy(
        src_ref=src, dst_ref=dst, send_sem=send, recv_sem=recv, device_id=device, device_id_type=MESH
    )


class Place:
    def __init__(self):
        self.row = lax.axis_index("row")
        self.col = lax.axis_index("col")
        self.y, self.x = self.row // NX, self.row % NX
        self.z, self.core = self.col // 2, self.col % 2
        self.sibling = (self.row, 2 * self.z + 1 - self.core)
        self.half, self.turn = self.row // 16, self.row % 16
        self.partner = (16 * self.half + self.col, self.turn)
        self.alone = self.turn == self.col

    def at_x(self, step):
        return (NX * self.y + (self.x + step) % NX, self.col)

    def at_y(self, step):
        return (NX * ((self.y + step) % NY) + self.x, self.col)

    def at_z(self, step):
        return (self.row, 2 * ((self.z + step) % NZ) + self.core)

    def greet(self):
        barrier = pltpu.get_barrier_semaphore()
        devices = [self.at_x(s) for s in range(1, NX)]
        devices += [self.at_y(s) for s in range(1, NY)]
        devices += [self.at_z(s) for s in range(1, NZ)]
        devices += [self.sibling]
        for device in devices:
            pl.semaphore_signal(barrier, inc=1, device_id=device, device_id_type=MESH)

        @pl.when(jnp.logical_not(self.alone))
        def _():
            pl.semaphore_signal(barrier, inc=1, device_id=self.partner, device_id_type=MESH)
            pl.semaphore_wait(barrier, len(devices) + 1)

        @pl.when(self.alone)
        def _():
            pl.semaphore_wait(barrier, len(devices))


class Ring:
    def __init__(self, count, me, device, slot, send, recv):
        self.count, self.me, self.device, self.slot = count, me, device, slot
        self.send, self.recv = send, recv

    def copy(self, step, arriving):
        owner = (self.me - step) % self.count if arriving else self.me
        ref = self.slot(owner)
        return remote(ref, ref, self.send.at[step], self.recv.at[step], self.device(step))

    def start(self):
        for step in sorted(range(1, self.count), key=lambda s: -min(s, self.count - s)):
            self.copy(step, False).start()

    def order(self):
        return sorted(range(1, self.count), key=lambda s: min(s, self.count - s))

    def wait_recv(self):
        for step in self.order():
            self.copy(step, True).wait_recv()

    def wait_send(self):
        for step in range(1, self.count):
            self.copy(step, False).wait_send()


class Line(Ring):
    def __init__(self, here, slot, send, recv, pass_send, pass_recv):
        super().__init__(NZ, here.z, here.at_z, lambda z: slot(2 * z + here.core), send, recv)
        self.here, self.across = here, lambda z: slot(2 * z + 1 - here.core)
        self.pass_send, self.pass_recv = pass_send, pass_recv

    def hand(self, step, arriving):
        owner = (self.me - step) % self.count
        ref = self.across(owner) if arriving else self.slot(owner)
        return remote(ref, ref, self.pass_send.at[step], self.pass_recv.at[step], self.here.sibling)

    def start(self):
        super().start()
        self.hand(0, False).start()

    def finish(self):
        for step in self.order():
            self.copy(step, True).wait_recv()
            self.hand(step, False).start()
        for step in [0] + self.order():
            self.hand(step, True).wait_recv()

    def wait_send(self):
        super().wait_send()
        for step in range(self.count):
            self.hand(step, False).wait_send()


def place_of(y):
    return 4 * ((y % 4) // 2) + 2 * (y // 4) + y % 2


class Spread:
    def __init__(self, here, buffer, swap, y_send, y_recv, x_send, x_recv):
        self.here, self.buffer, self.swap = here, buffer, swap
        self.ring = Ring(
            NY, here.y, here.at_y, lambda y: buffer.at[place_of(y), here.x], y_send, y_recv
        )
        self.x_send, self.x_recv = x_send, x_recv

    def swap_copy(self, source, arriving):
        here = self.here
        row = here.row if arriving else here.partner[0]
        target = self.buffer.at[place_of(row // NX), row % NX]
        return remote(source, target, self.swap.at[0], self.swap.at[1], here.partner)

    def start(self, source):
        here = self.here

        @pl.when(jnp.logical_not(here.alone))
        def _():
            self.swap_copy(source, False).start()

        @pl.when(here.alone)
        def _():
            self.buffer[place_of(here.y), here.x] = source[...]

    def along_y(self, source):
        @pl.when(jnp.logical_not(self.here.alone))
        def _():
            self.swap_copy(source, True).wait_recv()

        self.ring.start()

    def x_copy(self, index, arriving):
        here = self.here
        part = (0, 1, 1, 0, 0, 1)[index]
        step = (1, 1, -1, -1, 1, -1)[index]
        owner = here.x if index < 4 else (here.x - step) % NX
        if arriving:
            owner = (owner - step) % NX
        ref = self.buffer.at[pl.ds(4 * part, 4), owner]
        return remote(ref, ref, self.x_send.at[index], self.x_recv.at[index], here.at_x(step))

    def along_x(self):
        self.ring.wait_recv()
        for index in (0, 2, 1, 3):
            self.x_copy(index, False).start()

    def finish(self):
        for first, then in ((0, 4), (2, 5)):
            self.x_copy(first, True).wait_recv()
            self.x_copy(then, False).start()
        for index in (1, 3, 4, 5):
            self.x_copy(index, True).wait_recv()

    def wait_send(self, source):
        @pl.when(jnp.logical_not(self.here.alone))
        def _():
            self.swap_copy(source, False).wait_send()

        self.ring.wait_send()
        for index in range(6):
            self.x_copy(index, False).wait_send()


class Total:
    def __init__(self, here, over_x, over_y, whole, sems):
        self.here, self.over_x, self.over_y, self.whole = here, over_x, over_y, whole
        x_send, x_recv, y_send, y_recv, z_send, z_recv, p_send, p_recv = sems
        self.xs = Ring(NX, here.x, here.at_x, lambda x: over_x.at[x], x_send, x_recv)
        self.ys = Ring(NY, here.y, here.at_y, lambda y: over_y.at[y], y_send, y_recv)
        self.zs = Line(here, lambda c: whole.at[c], z_send, z_recv, p_send, p_recv)

    def along_x(self, value):
        self.over_x[self.here.x] = value
        self.xs.start()

    def along_y(self):
        self.xs.wait_recv()
        value = (self.over_x[0] + self.over_x[1]) + (self.over_x[2] + self.over_x[3])
        self.over_y[self.here.y] = value
        self.ys.start()

    def along_z(self):
        self.ys.wait_recv()
        parts = [self.over_y[y] for y in range(NY)]
        while len(parts) > 1:
            parts = [a + b for a, b in zip(parts[::2], parts[1::2])]
        self.whole[self.here.col] = parts[0]
        self.zs.start()

    def finish(self):
        self.zs.finish()

    def wait_send(self):
        self.xs.wait_send()
        self.ys.wait_send()
        self.zs.wait_send()


TOTAL_SEMS = [pltpu.SemaphoreType.DMA((n,)) for n in (NX, NX, NY, NY, NZ, NZ, NZ, NZ)]
LINE_SEMS = [pltpu.SemaphoreType.DMA((NZ,)) for _ in range(4)]
SPREAD_SEMS = [pltpu.SemaphoreType.DMA((n,)) for n in (2, NY, NY, 6, 6)]


def first_kernel(
    piece, square, slab, columns, gram, top, share, corner,
    whole, over_x, over_y, result, other, arrivals, own, pair, core_sems, back_send, back_recv, corner_send, corner_recv,
    top_send, top_recv, *sems
):
    here = Place()
    line = Line(here, lambda c: whole.at[c], *sems[:4])
    spread = Spread(here, columns, *sems[4:9])
    total = Total(here, over_x, over_y, gram, sems[9:17])
    tops = Line(here, lambda c: top.at[c], *sems[17:21])
    here.greet()

    whole[here.col] = piece[...]
    line.start()

    def corner_copy(z, index):
        return remote(
            square.at[pl.ds(2 * SLICE * z, 2 * SLICE), pl.ds(0, NB)], pair,
            corner_send.at[index], corner_recv.at[0], (here.row, 2 * z),
        )

    def corner_hand():
        return remote(
            pair.at[pl.ds(SLICE, SLICE), :], corner, corner_send.at[NZ], corner_recv.at[1], here.sibling
        )

    @pl.when(here.col == 0)
    def _():
        for z in range(1, NZ):
            corner_copy(z, z).start()
        pair[...] = square[pl.ds(0, 2 * SLICE), pl.ds(0, NB)]

    line.finish()
    flipped = whole[...].reshape(NB, 2 * NB)
    slab[...] = flipped.T
    own[...] = slab[pl.ds(pl.multiple_of(SLICE * here.col, SLICE), SLICE), :]
    spread.start(own)
    total.along_x(dot(piece[...], slab[...]))

    def top_x(step):
        ref = top.at[here.col]
        return remote(ref, ref, top_send.at[step], top_recv.at[0], here.at_x(step))

    def top_y(step):
        ref = top.at[here.col]
        return remote(ref, ref, top_send.at[NX + step], top_recv.at[1], here.at_y(step))

    @pl.when(here.row == 0)
    def _():
        top[here.col] = slab[pl.ds(pl.multiple_of(PIECE * here.col, PIECE), PIECE), :]
        for step in range(1, NX):
            top_x(step).start()

    spread.along_y(own)

    @pl.when(here.y == 0)
    def _():
        @pl.when(here.x > 0)
        def _():
            top_x(1).wait_recv()

        for step in range(1, NY):
            top_y(step).start()

    total.along_y()
    spread.along_x()

    @pl.when(here.y > 0)
    def _():
        top_y(1).wait_recv()

    tops.start()
    total.along_z()
    spread.finish()

    partial = dot(square[...], columns[...].reshape(4 * NB, NB))
    result[...] = partial.reshape(NZ, 2, SLICE, NB)
    across = remote(
        result.at[:, 1 - here.core], other, core_sems.at[0], core_sems.at[1], here.sibling
    )
    across.start()

    @pl.when(here.core == 0)
    def _():
        @pl.when(here.z > 0)
        def _():
            corner_copy(here.z, 0).wait_recv()

        corner_hand().start()
        corner[...] = pair[pl.ds(0, SLICE), :]

    tops.finish()
    total.finish()
    across.wait_recv()
    across.wait_send()

    mine = arrivals.at[0]

    def back(step):
        return remote(
            other.at[(here.z + step) % NZ], arrivals.at[step],
            back_send.at[step], back_recv.at[step], here.at_z(step),
        )

    for z in range(NZ):
        other[z] = other[z] + result[z, here.core]
    for step in (4, 3, 5, 2, 6, 1, 7):
        back(step).start()
    value = other[here.z]
    for step in (1, 7, 2, 6, 3, 5, 4):
        back(step).wait_recv()
        value = value + arrivals[step]
    share[...] = value

    for step in range(1, NZ):
        back(step).wait_send()

    @pl.when(here.col == 0)
    def _():
        for z in range(1, NZ):
            corner_copy(z, z).wait_send()

    @pl.when(here.core == 0)
    def _():
        corner_hand().wait_send()

    @pl.when(here.core == 1)
    def _():
        corner_hand().wait_recv()

    @pl.when(here.row == 0)
    def _():
        for step in range(1, NX):
            top_x(step).wait_send()

    @pl.when(here.y == 0)
    def _():
        for step in range(1, NY):
            top_y(step).wait_send()

    line.wait_send()
    spread.wait_send(own)
    total.wait_send()
    tops.wait_send()


def second_kernel(
    slab, share, corner, inverse, transform, update, vectors, columns,
    product, over_x, over_y, coupling, own, *sems
):
    here = Place()
    line = Line(here, lambda c: product.at[c], *sems[:4])
    spread = Spread(here, columns, *sems[4:9])
    total = Total(here, over_x, over_y, coupling, sems[9:17])
    here.greet()

    product[here.col] = dot(share[...], inverse[...], ((1,), (1,))) + corner[...]
    line.start()
    basis = dot(slab[...], inverse[...], ((1,), (1,)))
    at_top = here.row == 0
    rows = lax.broadcasted_iota(jnp.int32, basis.shape, 0)
    cols = lax.broadcasted_iota(jnp.int32, basis.shape, 1)
    vectors[...] = basis + jnp.where(jnp.logical_and(rows == cols, at_top), 1.0, 0.0)
    begin = pl.multiple_of(PIECE * here.col, PIECE)
    flipped = dot(inverse[pl.ds(begin, PIECE), :], slab[...], ((1,), (1,)))
    rows = lax.broadcasted_iota(jnp.int32, flipped.shape, 0) + begin
    cols = lax.broadcasted_iota(jnp.int32, flipped.shape, 1)
    flipped = flipped + jnp.where(jnp.logical_and(rows == cols, at_top), 1.0, 0.0)
    line.finish()
    whole = product[...].reshape(2 * NB, NB)
    total.along_x(dot(flipped, whole))
    scaled = dot(whole, transform[...])
    total.along_y()
    total.along_z()
    total.finish()
    inner = dot(coupling[...].reshape(NB, NB), transform[...])
    middle = dot(transform[...], inner, ((0,), (0,)))
    update[...] = scaled - 0.5 * dot(vectors[...], middle)
    own[...] = update[pl.ds(pl.multiple_of(SLICE * here.col, SLICE), SLICE), :]
    spread.start(own)
    spread.along_y(own)
    spread.along_x()
    spread.finish()

    line.wait_send()
    spread.wait_send(own)
    total.wait_send()


def vmem(*shape):
    return jax.ShapeDtypeStruct(shape, jnp.float32)


def kernel_call(body, name, ident, outs, scratch, *args):
    whole = pl.BlockSpec(memory_space=pltpu.VMEM)
    return pl.pallas_call(
        body,
        out_shape=[vmem(*s) for s in outs],
        in_specs=[whole] * len(args),
        out_specs=[whole] * len(outs),
        scratch_shapes=scratch,
        compiler_params=pltpu.CompilerParams(
            collective_id=ident, has_side_effects=True, vmem_limit_bytes=VMEM_LIMIT
        ),
        name=name,
    )(*args)


def scratch(*shape):
    return pltpu.VMEM(shape, jnp.float32)


def dma(n):
    return pltpu.SemaphoreType.DMA((n,))


def matmul(left, right):
    return jnp.dot(left, right, preferred_element_type=jnp.float32, precision=precise)


def invert(square):
    normal = matmul(square.T, square)
    factor = jnp.linalg.cholesky(normal)
    middle = lax.linalg.triangular_solve(factor, square.T, left_side=True, lower=True)
    return lax.linalg.triangular_solve(factor, middle, left_side=True, lower=True, transpose_a=True)


def per_device(panel, matrix):
    square = matrix.reshape(2 * NB, 4 * NB)
    piece = panel.reshape(2 * NB, PIECE).T
    slab, columns, gram, top, share, corner = kernel_call(
        first_kernel, "first", 0,
        [(2 * NB, NB), (8, 4, SLICE, NB), (PIECE, PIECE, NB), (PIECE, PIECE, NB), (SLICE, NB), (SLICE, NB)],
        [
            scratch(PIECE, PIECE, 2 * NB), scratch(NX, PIECE, NB), scratch(NY, PIECE, NB),
            scratch(NZ, 2, SLICE, NB), scratch(NZ, SLICE, NB), scratch(NZ, SLICE, NB), scratch(SLICE, NB), scratch(2 * SLICE, NB),
            dma(2), dma(NZ), dma(NZ), dma(NZ + 1), dma(2), dma(NX + NY), dma(2),
            *LINE_SEMS, *SPREAD_SEMS, *TOTAL_SEMS, *LINE_SEMS,
        ],
        piece, square,
    )
    columns = columns.reshape(4 * NB, NB)
    identity = jnp.eye(NB, dtype=jnp.float32)
    lower_one = jnp.linalg.cholesky(gram.reshape(NB, NB))
    inverse = lax.linalg.triangular_solve(lower_one, identity, left_side=True, lower=True)
    leading = matmul(top.reshape(NB, NB), inverse.T)
    transform = invert(identity + leading.T)
    update, vectors, update_cols = kernel_call(
        second_kernel, "second", 1,
        [(2 * NB, NB), (2 * NB, NB), (8, 4, SLICE, NB)],
        [
            scratch(PIECE, SLICE, NB), scratch(NX, PIECE, NB), scratch(NY, PIECE, NB),
            scratch(PIECE, PIECE, NB), scratch(SLICE, NB),
            *LINE_SEMS, *SPREAD_SEMS, *TOTAL_SEMS,
        ],
        slab, share, corner, inverse, transform,
    )
    update_cols = update_cols.reshape(4 * NB, NB)
    first = (lax.axis_index("col") == 0).astype(jnp.float32)
    vectors_cols = dot(columns, inverse, ((1,), (1,))).at[:NB].add(identity * first)
    left = jnp.concatenate([update, vectors], axis=1)
    right = jnp.concatenate([vectors_cols, update_cols], axis=1)
    updated = square - dot(left, right, ((1,), (1,)))
    return (updated.reshape(matrix.shape), lower_one.T)


def solution(mesh):
    in_specs = (P(None, "row", "col"), P(None, "row", None, "col"))
    out_specs = (P(None, "row", None, "col"), P())
    return jax.shard_map(
        per_device, mesh=mesh, in_specs=in_specs, out_specs=out_specs, check_vma=False
    )
```

time: 955 us -> 288 us (0.30); the launches traced: 938 us -> 284 us
  waiting for transfers between devices: 722 us -> 0 us
  Pallas kernels: 0 us -> 120 us
  blocking collectives: 26.2 us -> 0 us
  matrix products: 31.5 us -> 17.6 us
  between operations: 17 us -> 3.76 us
    psum x5 -> x0, waiting for transfers between devices: 722 us -> none  [the longest x2 309 us: from_root(): return lax.psum(block, axis)]
    pallas_call x0 -> x2, Pallas kernels: none -> 120 us  [kernel_call(): pl.pallas_call(body, out_shape=[vmem(*s) for s in outs], in_specs=[whole]...]
    all_gather x1 -> x0, blocking collectives: 26.2 us -> none  [per_device(): lax.all_gather(panel, 'col', axis=2, tiled=True)]
    dot_general x5 -> x2, matrix products: 12.2 us -> 1.01 us  [matmul(): jnp.dot(left, right, preferred_element_type=jnp.float32, precision=precise)]
    another operation x11 -> x9, other arithmetic: 56.4 us -> 56.7 us  [the longest x6 35.5 us: per_device(): lower_one = jnp.linalg.cholesky(gram.reshape(NB, NB))]
    another operation x2 -> x3, other arithmetic: 19.7 us -> 19.7 us  [invert(): lax.linalg.triangular_solve(factor, middle, left_side=True, lower=True, t...]
  transfers between devices with their start and end apart: 5 -> 0, of which waited for: 5 -> 0; matrix products, arithmetic and copies ran while one was open for 1% -> 0% of each run, Pallas kernels for 0% -> 0%
where the time goes in v1:
time: 288 us; the launch traced here: 284 us
  Pallas kernels  120 us (42%)
  other arithmetic  115 us (40%)
  local copies, waits for them, and re-layouts  27.5 us (10%)
  matrix products  17.6 us (6%)
  between operations  3.76 us (1%)
    pallas_call x2, Pallas kernels, kernel_call(): pl.pallas_call(body, out_shape=[vmem(*s) for s in outs], in_specs=[whole]...  120 us
    another operation x6, other arithmetic, per_device(): lower_one = jnp.linalg.cholesky(gram.reshape(NB, NB))  35.5 us
    another operation x7, other arithmetic, invert(): factor = jnp.linalg.cholesky(normal)  34.8 us
    another operation x3, other arithmetic, per_device(): lax.linalg.triangular_solve(lower_one, identity, left_side=True, lower=True)  21.3 us
    another operation x3, other arithmetic, invert(): lax.linalg.triangular_solve(factor, middle, left_side=True, lower=True, t...  19.7 us
    unnamed x23, local copies, waits for them, and re-layouts  10.4 us
    dot_general x2, matrix products, dot(): lax.dot_general(left, right, (contract, ((), ())), preferred_element_type...  7.83 us
    another operation x9, local copies, waits for them, and re-layouts, per_device(): lax.linalg.triangular_solve(lower_one, identity, left_side=True, lower=True)  6.02 us

profile of v1, /device:TPU:1, one launch (start us, length us, event | category | flops | bytes accessed | tf_op | source)
XLA Modules:
  0.0 284.0 jit_solution(3556270860662644860)
XLA Ops:
  2.2 2.1 copy.21
  4.2 62.4 %first.1 = (f32[512,256]{1,0:T(8,128)S(1)}, f32[8,4,32,256]{3,2,1,0:T(8,128)S(1)}, f32[16,16,256]{2,1,0:T(8,128)S(1)}, f32[16,16,256]{2,1,0:T(8,128)S(1)}, f32[32,256]{1,0:T(8,128)S(1)}, /*index=5*/f32[32,256]{1,0:T(8,128)S(1)}) custom-call(f32[16,512]{1,0:T(8,128)S(1)} %bitcast.96, f32[512,1024]{1,0:T(8,128)S(1)} %bitcast.90), custom_call_target="tpu_custom_call" | custom-call | tf_op jit(solution)/shard_map/first/pallas_call | solution.py:427
  68.1 0.8 copy.13
  68.9 1.0 fusion.11
  70.6 11.7 %cholesky.130 = f32[128,128]{1,0:T(8,128)S(1)} custom-call(f32[128,128]{1,0:T(8,128)S(1)} %cholesky.194), custom_call_target="Cholesky" | custom-call | tf_op jit(solution)/shard_map/jit(cholesky)/cholesky | solution.py:475
  82.4 10.4 %custom-call.17 = f32[1,128,128]{1,2,0:T(8,128)} custom-call(f32[1,128,128]{2,1,0:T(8,128)S(1)} %get-tuple-element.91), custom_call_target="InvertDiagBlocksLowerTriangular" | custom-call | tf_op jit(solution)/shard_map/jit(cholesky)/cholesky | solution.py:475
  92.8 1.1 constant_dynamic-update-slice_fusion.2
  93.9 1.7 convolution_subtract_fusion.4
  95.7 12.5 %cholesky.147 = f32[128,128]{1,0:T(8,128)S(1)} custom-call(f32[128,128]{1,0:T(8,128)} %convolution_subtract_fusion.4), custom_call_target="Cholesky" | custom-call | tf_op jit(solution)/shard_map/jit(cholesky)/cholesky | solution.py:475
  110.3 1.7 fusion.17
  112.0 1.8 copy.18
  114.4 5.3 %while.7 = (s32[]{:T(128)}, f32[256,256]{1,0:T(8,128)S(1)}, s32[2,2]{1,0:T(2,128)S(1)}, f32[2,128,128]{2,1,0:T(8,128)}, s32[]{:T(128)}) while((s32[]{:T(128)}, f32[256,256]{1,0:T(8,128)S(1)}, s32[2,2]{1,0:T(2,128)S(1)}, f32[2,128,128]{2,1,0:T(8,128)}, s32[]{:T(128)}) %tuple.58), condition=%wide.while_cond.1, body=%wide.while_body.1.sunk | while | flops 2 | bytes 132205 | solution.py:476
  115.0 2.0 bitcast_dynamic-update-slice_fusion.5
  117.7 2.0 bitcast_dynamic-update-slice_fusion.5
  120.4 21.2 %custom-call.18 = f32[2,128,128]{1,2,0:T(8,128)} custom-call(f32[2,128,128]{2,1,0:T(8,128)} %get-tuple-element.56), custom_call_target="InvertDiagBlocksLowerTriangular" | custom-call | tf_op jit(solution)/shard_map/triangular_solve/custom-call.0 | solution.py:476
  141.6 1.3 fusion.20
  142.9 1.2 convolution_subtract_fusion.2
  144.1 1.1 fusion.26
  145.3 1.1 fusion.37
  146.3 1.0 copy-done.6
  149.7 11.7 %cholesky.164 = f32[128,128]{1,0:T(8,128)S(1)} custom-call(f32[128,128]{1,0:T(8,128)S(1)} %cholesky.197), custom_call_target="Cholesky" | custom-call | tf_op jit(solution)/shard_map/jit(cholesky)/cholesky | solution.py:454
  162.1 9.8 %custom-call.19 = f32[1,128,128]{1,2,0:T(8,128)S(1)} custom-call(f32[1,128,128]{2,1,0:T(8,128)S(1)} %get-tuple-element.87), custom_call_target="InvertDiagBlocksLowerTriangular" | custom-call | tf_op jit(solution)/shard_map/jit(cholesky)/cholesky | solution.py:454
  172.4 11.9 %cholesky.181 = f32[128,128]{1,0:T(8,128)S(1)} custom-call(f32[128,128]{1,0:T(8,128)S(1)} %convolution_subtract_fusion.3), custom_call_target="Cholesky" | custom-call | tf_op jit(solution)/shard_map/jit(cholesky)/cholesky | solution.py:454
  186.3 3.9 %while.6 = (s32[]{:T(128)}, f32[256,256]{1,0:T(8,128)S(1)}, s32[2,2]{1,0:T(2,128)S(1)}, f32[2,128,128]{2,1,0:T(8,128)S(1)}, s32[]{:T(128)}) while((s32[]{:T(128)}, f32[256,256]{1,0:T(8,128)S(1)}, s32[2,2]{1,0:T(2,128)S(1)}, f32[2,128,128]{2,1,0:T(8,128)S(1)}, s32[]{:T(128)}) %tuple.64), condition=%wide.while_cond.2, body=%wide.while_body.2.sunk | while | flops 2 | bytes 131189 | solution.py:456
  187.0 1.3 bitcast_dynamic-update-slice_fusion.4
  188.9 1.3 bitcast_dynamic-update-slice_fusion.4
  190.2 19.7 %custom-call.14 = f32[2,128,128]{1,2,0:T(8,128)S(1)} custom-call(f32[2,128,128]{2,1,0:T(8,128)S(1)} %get-tuple-element.49), custom_call_target="InvertDiagBlocksLowerTriangular" | custom-call | tf_op jit(solution)/shard_map/triangular_solve | solution.py:456
  211.8 1.0 copy-done.3
  212.9 58.1 %second.1 = (f32[512,256]{1,0:T(8,128)S(1)}, f32[512,256]{1,0:T(8,128)S(1)}, f32[8,4,32,256]{3,2,1,0:T(8,128)S(1)}) custom-call(f32[512,256]{1,0:T(8,128)S(1)} %copy-done.3, f32[32,256]{1,0:T(8,128)S(1)} %get-tuple-element.26.share, f32[32,256]{1,0:T(8,128)S(1)} %get-tuple-element.27.corner, f32[256,256]{1,0:T(8,128)S(1)} %pad_maximum_fusion.inverse, ...), custom_call_target="tpu_custom_call" | custom-call | tf_op jit(solution)/shard_map/second/pallas_call | solution.py:427
  272.5 1.3 copy.17
  273.8 6.8 %fusion.4 = f32[512,1024]{1,0:T(8,128)} fusion(f32[512,1024]{1,0:T(8,128)S(1)} %bitcast.91, f32[1024,256]{0,1:T(8,128)} %copy.17, f32[1024,256]{0,1:T(8,128)} %constant_dynamic-update-slice_fusion.4, f32[512,256]{1,0:T(8,128)} %copy-done.1, f32[512,256]{1,0:T(8,128)} %copy-done), kind=kOutput, calls=%fused_computation.8 | convolution fusion | flops 3222536192 | bytes 7340032 | tf_op jit(solution)/shard_map/dot_general | solution.py:20
  280.6 3.2 %reshape.78 = f32[2,256,4,256]{3,2,1,0:T(4,128)} reshape(f32[512,1024]{1,0:T(8,128)} %fusion.4) | data formatting | bytes 4194304 | tf_op jit(solution)/shard_map/reshape | solution.py:495
  (63 shorter events, 16.1 us)
Async XLA Ops:
  66.6 0.8 copy-start.2
  67.4 0.7 copy-start.4
  69.9 0.7 copy-start.9
  108.2 0.7 copy-start.8
  119.7 0.7 copy-start.7
  146.3 1.0 copy-start.6
  147.3 1.1 copy-start.5
  211.8 1.0 copy-start.3
  270.9 0.8 copy-start
  271.7 0.8 copy-start.1

commit v2 on v1

--- a/solution.py
+++ b/solution.py
@@ -418,6 +418,82 @@
     total.wait_send()
 
 
+LANES, GROUP, STEP = 128, 32, 8
+
+
+def columns_of(block, begin, rows):
+    return [jnp.broadcast_to(block[:, begin + l : begin + l + 1], (rows, LANES)) for l in range(STEP)]
+
+
+def factor_kernel(gram, top, upper, inverse, transform, work, pad):
+    lane = lax.broadcasted_iota(jnp.int32, (GROUP, LANES), 1)
+    line = lax.broadcasted_iota(jnp.int32, (GROUP, LANES), 0)
+    rows_all = lax.broadcasted_iota(jnp.int32, (NB, NB), 0)
+    cols_all = lax.broadcasted_iota(jnp.int32, (NB, NB), 1)
+    identity = jnp.where(rows_all == cols_all, 1.0, 0.0)
+    work[:, :NB] = gram[...]
+    work[:, NB:] = identity
+    for base in range(0, NB, GROUP):
+        first, last = base // LANES, 2 + base // LANES + 1
+        blocks = {q: work[base : base + GROUP, LANES * q : LANES * (q + 1)] for q in range(first, last)}
+        for sub in range(0, GROUP, STEP):
+            count = GROUP - sub
+            number = line[:count]
+            cols = columns_of(blocks[first], (base + sub) % LANES, count)
+            scale = jnp.ones((STEP, LANES), jnp.float32)
+            for j in range(STEP):
+                pivot = cols[j][j : j + 1]
+                over = 1.0 / pivot
+                scale = jnp.where(number[:STEP] == j, lax.rsqrt(pivot), scale)
+                factor = jnp.where(number > j, cols[j] * over, 0.0)
+                for l in range(j + 1, STEP):
+                    cols[l] = cols[l] - factor * cols[l][j : j + 1]
+                for q in blocks:
+                    blocks[q] = blocks[q] - factor * blocks[q][j : j + 1]
+            for q in blocks:
+                work[base + sub : base + sub + STEP, LANES * q : LANES * (q + 1)] = blocks[q][:STEP] * scale
+                blocks[q] = blocks[q][STEP:]
+        after = base + GROUP
+        if after < NB:
+            start = after // LANES
+            left = work[base:after, LANES * start : NB]
+            right = work[base:after, LANES * start : LANES * last]
+            change = dot(left, right, ((0,), (0,)))
+            work[after:, LANES * start : LANES * last] -= change[after - LANES * start :]
+    upper[...] = jnp.where(rows_all <= cols_all, work[:, :NB], 0.0)
+    inverse[...] = work[:, NB:]
+    transform[...] = dot(inverse[...], top[...], ((1,), (1,))) + identity
+    pad[...] = jnp.zeros_like(pad)
+    lane_all = lax.broadcasted_iota(jnp.int32, (NB, LANES), 1)
+    for base in range(0, NB, GROUP):
+        home, offset = base // LANES, base % LANES
+        blocks = {q: transform[base : base + GROUP, LANES * q : LANES * (q + 1)] for q in range(2)}
+        blocks[2] = jnp.where(lane == line + offset, 1.0, 0.0)
+        scale = jnp.ones((GROUP, LANES), jnp.float32)
+        for sub in range(0, GROUP, STEP):
+            cols = columns_of(blocks[home], offset + sub, GROUP)
+            for j in range(STEP):
+                row = sub + j
+                over = 1.0 / cols[j][row : row + 1]
+                scale = jnp.where(line == row, over, scale)
+                factor = jnp.where(line == row, 0.0, cols[j] * over)
+                for l in range(j + 1, STEP):
+                    cols[l] = cols[l] - factor * cols[l][row : row + 1]
+                for q in blocks:
+                    blocks[q] = blocks[q] - factor * blocks[q][row : row + 1]
+        inside = jnp.logical_and(lane >= offset, lane < offset + GROUP)
+        blocks = {q: blocks[q] * scale for q in blocks}
+        blocks[home] = jnp.where(inside, blocks[2], blocks[home])
+        for q in range(2):
+            pad[offset : offset + GROUP, LANES * q : LANES * (q + 1)] = blocks[q]
+        mine = transform[:, LANES * home : LANES * (home + 1)]
+        inside_all = jnp.logical_and(lane_all >= offset, lane_all < offset + GROUP)
+        change = dot(jnp.where(inside_all, mine, 0.0), pad[...])
+        transform[:, LANES * home : LANES * (home + 1)] = jnp.where(inside_all, 0.0, mine)
+        transform[...] -= change
+        transform[base : base + GROUP, :] = pad[offset : offset + GROUP, :]
+        pad[offset : offset + GROUP, :] = jnp.zeros((GROUP, NB), jnp.float32)
+
 def vmem(*shape):
     return jax.ShapeDtypeStruct(shape, jnp.float32)
 
@@ -445,15 +521,17 @@
     return pltpu.SemaphoreType.DMA((n,))
 
 
-def matmul(left, right):
-    return jnp.dot(left, right, preferred_element_type=jnp.float32, precision=precise)
-
-
-def invert(square):
-    normal = matmul(square.T, square)
-    factor = jnp.linalg.cholesky(normal)
-    middle = lax.linalg.triangular_solve(factor, square.T, left_side=True, lower=True)
-    return lax.linalg.triangular_solve(factor, middle, left_side=True, lower=True, transpose_a=True)
+def factor(gram, top):
+    whole = pl.BlockSpec(memory_space=pltpu.VMEM)
+    return pl.pallas_call(
+        factor_kernel,
+        out_shape=[vmem(NB, NB)] * 3,
+        in_specs=[whole] * 2,
+        out_specs=[whole] * 3,
+        scratch_shapes=[scratch(NB, 2 * NB), scratch(LANES, NB)],
+        compiler_params=pltpu.CompilerParams(vmem_limit_bytes=VMEM_LIMIT),
+        name="factor",
+    )(gram, top)
 
 
 def per_device(panel, matrix):
@@ -472,10 +550,7 @@
     )
     columns = columns.reshape(4 * NB, NB)
     identity = jnp.eye(NB, dtype=jnp.float32)
-    lower_one = jnp.linalg.cholesky(gram.reshape(NB, NB))
-    inverse = lax.linalg.triangular_solve(lower_one, identity, left_side=True, lower=True)
-    leading = matmul(top.reshape(NB, NB), inverse.T)
-    transform = invert(identity + leading.T)
+    upper, inverse, transform = factor(gram.reshape(NB, NB), top.reshape(NB, NB))
     update, vectors, update_cols = kernel_call(
         second_kernel, "second", 1,
         [(2 * NB, NB), (2 * NB, NB), (8, 4, SLICE, NB)],
@@ -492,7 +567,7 @@
     left = jnp.concatenate([update, vectors], axis=1)
     right = jnp.concatenate([vectors_cols, update_cols], axis=1)
     updated = square - dot(left, right, ((1,), (1,)))
-    return (updated.reshape(matrix.shape), lower_one.T)
+    return (updated.reshape(matrix.shape), upper)
 
 
 def solution(mesh):

time: 288 us -> 158 us (0.55); the launches traced: 284 us -> 158 us
  other arithmetic: 115 us -> 0.07 us
  Pallas kernels: 120 us -> 141 us
  local copies, waits for them, and re-layouts: 27.5 us -> 8.87 us
  matrix products: 17.6 us -> 7.82 us
  between operations: 3.76 us -> 0.7 us
    another operation x19 -> x0, other arithmetic: 111 us -> none  [the longest x6 35.5 us: per_device(): lower_one = jnp.linalg.cholesky(gram.reshape(NB, NB))]
    pallas_call x0 -> x1, Pallas kernels: none -> 20.7 us  [factor(): pl.pallas_call(factor_kernel, out_shape=[vmem(NB, NB)] * 3, in_specs=[who...]
    another operation x20 -> x0, local copies, waits for them, and re-layouts: 9.98 us -> none  [the longest x9 6.02 us: per_device(): lax.linalg.triangular_solve(lower_one, identity, left_side=True, lower=True)]
    another operation x13 -> x0, matrix products: 8.73 us -> none  [the longest x3 3.61 us: per_device(): lax.linalg.triangular_solve(lower_one, identity, left_side=True, lower=True)]
    unnamed x23 -> x7, local copies, waits for them, and re-layouts: 10.4 us -> 3.65 us
where the time goes in v2:
time: 158 us
  Pallas kernels  141 us (89%)
  local copies, waits for them, and re-layouts  8.87 us (6%)
  matrix products  7.82 us (5%)
    pallas_call x2, Pallas kernels, kernel_call(): pl.pallas_call(body, out_shape=[vmem(*s) for s in outs], in_specs=[whole]...  120 us
    pallas_call x1, Pallas kernels, factor(): pl.pallas_call(factor_kernel, out_shape=[vmem(NB, NB)] * 3, in_specs=[who...  20.7 us
    dot_general x2, matrix products, dot(): lax.dot_general(left, right, (contract, ((), ())), preferred_element_type...  7.82 us
    unnamed x7, local copies, waits for them, and re-layouts  3.65 us

profile of v2, /device:TPU:1, one launch (start us, length us, event | category | flops | bytes accessed | tf_op | source)
XLA Modules:
  0.0 158.2 jit_solution(14145207415725099265)
XLA Ops:
  0.6 0.8 copy.6
  1.4 2.1 %copy.7 = f32[64,8,4,256]{3,1,2,0:T(8,128)S(1)} copy(f32[64,8,4,256]{3,2,1,0:T(4,128)} %bitcast.20) | data formatting | bytes 4194304
  3.5 62.2 %first.1 = (f32[512,256]{1,0:T(8,128)S(1)}, f32[8,4,32,256]{3,2,1,0:T(8,128)S(1)}, f32[16,16,256]{2,1,0:T(8,128)S(1)}, f32[16,16,256]{2,1,0:T(8,128)S(1)}, f32[32,256]{1,0:T(8,128)S(1)}, /*index=5*/f32[32,256]{1,0:T(8,128)S(1)}) custom-call(f32[16,512]{1,0:T(8,128)S(1)} %bitcast.19, f32[512,1024]{1,0:T(8,128)S(1)} %bitcast.13), custom_call_target="tpu_custom_call" | custom-call | tf_op jit(solution)/shard_map/first/pallas_call | solution.py:503
  65.7 20.7 %factor.1 = (f32[256,256]{1,0:T(8,128)}, f32[256,256]{1,0:T(8,128)S(1)}, f32[256,256]{1,0:T(8,128)S(1)}) custom-call(f32[256,256]{1,0:T(8,128)S(1)} %bitcast.17, f32[256,256]{1,0:T(8,128)S(1)} %bitcast.18), custom_call_target="tpu_custom_call" | custom-call | tf_op jit(solution)/shard_map/factor/pallas_call | solution.py:526
  86.4 1.1 fusion.12
  87.5 0.1 fusion.10
  87.6 0.0 copy-start.2
  87.6 57.8 %second.1 = (f32[512,256]{1,0:T(8,128)S(1)}, f32[512,256]{1,0:T(8,128)S(1)}, f32[8,4,32,256]{3,2,1,0:T(8,128)S(1)}) custom-call(f32[512,256]{1,0:T(8,128)S(1)} %get-tuple-element.26.slab, f32[32,256]{1,0:T(8,128)S(1)} %get-tuple-element.27.share, f32[32,256]{1,0:T(8,128)S(1)} %get-tuple-element.28.corner, f32[256,256]{1,0:T(8,128)S(1)} %get-tuple-element.31.inverse, ...), custom_call_target="tpu_custom_call" | custom-call | tf_op jit(solution)/shard_map/second/pallas_call | solution.py:503
  145.4 0.0 copy-done.2
  145.4 0.0 copy-start
  145.4 0.8 copy-done
  146.2 0.0 copy-start.1
  146.2 0.8 copy-done.1
  147.0 1.3 copy.5
  148.3 6.8 %fusion.4 = f32[512,1024]{1,0:T(8,128)} fusion(f32[512,1024]{1,0:T(8,128)S(1)} %bitcast.14, f32[1024,256]{0,1:T(8,128)} %copy.5, f32[1024,256]{0,1:T(8,128)} %copy-done.2, f32[512,256]{1,0:T(8,128)} %copy-done.1, f32[512,256]{1,0:T(8,128)} %copy-done), kind=kOutput, calls=%fused_computation.4 | convolution fusion | flops 3222536192 | bytes 7340032 | tf_op jit(solution)/shard_map/dot_general | solution.py:20
  155.0 3.2 %reshape.57 = f32[2,256,4,256]{3,2,1,0:T(4,128)} reshape(f32[512,1024]{1,0:T(8,128)} %fusion.4) | data formatting | bytes 4194304 | tf_op jit(solution)/shard_map/reshape | solution.py:570
Async XLA Ops:
  87.6 57.8 %copy-start.2 = (f32[1024,256]{0,1:T(8,128)}, f32[1024,256]{0,1:T(8,128)S(1)}, u32[]{:S(2)}) copy-start(f32[1024,256]{0,1:T(8,128)S(1)} %fusion.10) | copy-start | bytes 3145732
  145.4 0.8 copy-start
  146.2 0.8 copy-start.1

commit v3 on v1

v3 whole, which is shorter than its diff:
```python
import functools

import jax
import jax.numpy as jnp
from jax import lax
from jax.experimental import pallas as pl
from jax.experimental.pallas import tpu as pltpu
from jax.sharding import PartitionSpec as P

MESH = pl.DeviceIdType.MESH
precise = lax.Precision.HIGHEST
NX, NY, NZ = 4, 8, 8
NB = 256
PIECE = 16
SLICE = 32
VMEM_LIMIT = 40 * 1024 * 1024


def dot(left, right, contract=((1,), (0,))):
    return lax.dot_general(
        left, right, (contract, ((), ())), preferred_element_type=jnp.float32, precision=precise
    )


def remote(src, dst, send, recv, device):
    return pltpu.make_async_remote_copy(
        src_ref=src, dst_ref=dst, send_sem=send, recv_sem=recv, device_id=device, device_id_type=MESH
    )


class Place:
    def __init__(self):
        self.row = lax.axis_index("row")
        self.col = lax.axis_index("col")
        self.y, self.x = self.row // NX, self.row % NX
        self.z, self.core = self.col // 2, self.col % 2
        self.sibling = (self.row, 2 * self.z + 1 - self.core)
        self.half, self.turn = self.row // 16, self.row % 16
        self.partner = (16 * self.half + self.col, self.turn)
        self.alone = self.turn == self.col

    def at_x(self, step):
        return (NX * self.y + (self.x + step) % NX, self.col)

    def at_y(self, step):
        return (NX * ((self.y + step) % NY) + self.x, self.col)

    def at_z(self, step):
        return (self.row, 2 * ((self.z + step) % NZ) + self.core)

    def greet(self):
        barrier = pltpu.get_barrier_semaphore()
        devices = [self.at_x(s) for s in range(1, NX)]
        devices += [self.at_y(s) for s in range(1, NY)]
        devices += [self.at_z(s) for s in range(1, NZ)]
        devices += [self.sibling]
        for device in devices:
            pl.semaphore_signal(barrier, inc=1, device_id=device, device_id_type=MESH)

        @pl.when(jnp.logical_not(self.alone))
        def _():
            pl.semaphore_signal(barrier, inc=1, device_id=self.partner, device_id_type=MESH)
            pl.semaphore_wait(barrier, len(devices) + 1)

        @pl.when(self.alone)
        def _():
            pl.semaphore_wait(barrier, len(devices))


class Ring:
    def __init__(self, count, me, device, slot, send, recv):
        self.count, self.me, self.device, self.slot = count, me, device, slot
        self.send, self.recv = send, recv

    def copy(self, step, arriving):
        owner = (self.me - step) % self.count if arriving else self.me
        ref = self.slot(owner)
        return remote(ref, ref, self.send.at[step], self.recv.at[step], self.device(step))

    def start(self):
        for step in sorted(range(1, self.count), key=lambda s: -min(s, self.count - s)):
            self.copy(step, False).start()

    def order(self):
        return sorted(range(1, self.count), key=lambda s: min(s, self.count - s))

    def wait_recv(self):
        for step in self.order():
            self.copy(step, True).wait_recv()

    def wait_send(self):
        for step in range(1, self.count):
            self.copy(step, False).wait_send()


class Line(Ring):
    def __init__(self, here, slot, send, recv, pass_send, pass_recv):
        super().__init__(NZ, here.z, here.at_z, lambda z: slot(2 * z + here.core), send, recv)
        self.here, self.across = here, lambda z: slot(2 * z + 1 - here.core)
        self.pass_send, self.pass_recv = pass_send, pass_recv

    def hand(self, step, arriving):
        owner = (self.me - step) % self.count
        ref = self.across(owner) if arriving else self.slot(owner)
        return remote(ref, ref, self.pass_send.at[step], self.pass_recv.at[step], self.here.sibling)

    def start(self):
        super().start()
        self.hand(0, False).start()

    def finish(self):
        for step in self.order():
            self.copy(step, True).wait_recv()
            self.hand(step, False).start()
        for step in [0] + self.order():
            self.hand(step, True).wait_recv()

    def wait_send(self):
        super().wait_send()
        for step in range(self.count):
            self.hand(step, False).wait_send()


def place_of(y):
    return 4 * ((y % 4) // 2) + 2 * (y // 4) + y % 2


class Spread:
    def __init__(self, here, buffer, y_send, y_recv, x_send, x_recv):
        self.here, self.buffer = here, buffer
        self.ring = Ring(
            NY, here.y, here.at_y, lambda y: buffer.at[place_of(y), here.x], y_send, y_recv
        )
        self.x_send, self.x_recv = x_send, x_recv

    def along_y(self):
        self.ring.start()

    def x_copy(self, index, arriving):
        here = self.here
        part = (0, 1, 1, 0, 0, 1)[index]
        step = (1, 1, -1, -1, 1, -1)[index]
        owner = here.x if index < 4 else (here.x - step) % NX
        if arriving:
            owner = (owner - step) % NX
        ref = self.buffer.at[pl.ds(4 * part, 4), owner]
        return remote(ref, ref, self.x_send.at[index], self.x_recv.at[index], here.at_x(step))

    def along_x(self):
        self.ring.wait_recv()
        for index in (0, 2, 1, 3):
            self.x_copy(index, False).start()

    def forward(self):
        for first, then in ((0, 4), (2, 5)):
            self.x_copy(first, True).wait_recv()
            self.x_copy(then, False).start()

    def finish(self):
        for index in (1, 3, 4, 5):
            self.x_copy(index, True).wait_recv()

    def wait_send(self):
        self.ring.wait_send()
        for index in range(6):
            self.x_copy(index, False).wait_send()


class Swap:
    def __init__(self, here, source, target_at, sems):
        self.here, self.source, self.target_at, self.sems = here, source, target_at, sems

    def copy(self, arriving):
        here = self.here
        target = self.target_at(*((here.row, here.col) if arriving else here.partner))
        return remote(self.source, target, self.sems.at[0], self.sems.at[1], here.partner)

    def start(self):
        @pl.when(jnp.logical_not(self.here.alone))
        def _():
            self.copy(False).start()

        @pl.when(self.here.alone)
        def _():
            self.target_at(self.here.row, self.here.col)[...] = self.source[...]

    def wait_recv(self):
        @pl.when(jnp.logical_not(self.here.alone))
        def _():
            self.copy(True).wait_recv()

    def wait_send(self):
        @pl.when(jnp.logical_not(self.here.alone))
        def _():
            self.copy(False).wait_send()


class Total:
    def __init__(self, here, over_x, over_y, whole, sems):
        self.here, self.over_x, self.over_y, self.whole = here, over_x, over_y, whole
        x_send, x_recv, y_send, y_recv, z_send, z_recv, p_send, p_recv = sems
        self.xs = Ring(NX, here.x, here.at_x, lambda x: over_x.at[x], x_send, x_recv)
        self.ys = Ring(NY, here.y, here.at_y, lambda y: over_y.at[y], y_send, y_recv)
        self.zs = Line(here, lambda c: whole.at[c], z_send, z_recv, p_send, p_recv)

    def along_x(self, value):
        self.over_x[self.here.x] = value
        self.xs.start()

    def along_y(self):
        self.xs.wait_recv()
        value = (self.over_x[0] + self.over_x[1]) + (self.over_x[2] + self.over_x[3])
        self.over_y[self.here.y] = value
        self.ys.start()

    def along_z(self):
        self.ys.wait_recv()
        parts = [self.over_y[y] for y in range(NY)]
        while len(parts) > 1:
            parts = [a + b for a, b in zip(parts[::2], parts[1::2])]
        self.whole[self.here.col] = parts[0]
        self.zs.start()

    def finish(self):
        self.zs.finish()

    def wait_send(self):
        self.xs.wait_send()
        self.ys.wait_send()
        self.zs.wait_send()


class PlaneSum:
    def __init__(self, here, terms, early, late, kept, arrivals, x_send, x_recv, y_send, y_recv):
        self.here, self.terms, self.early, self.late = here, terms, early, late
        self.kept, self.arrivals = kept, arrivals
        self.x_send, self.x_recv, self.y_send, self.y_recv = x_send, x_recv, y_send, y_recv

    def x_copy(self, index):
        here, way = self.here, index % 2
        step = 1 - 2 * way
        half = (way, 1 - way, way)[index // 2]
        owner = (here.x + (2 if index < 2 else step)) % NX
        source = self.terms.at[pl.ds(4 * half, 4), owner]
        target = self.early.at[way] if index < 2 else self.late.at[way, pl.ds(4 * half, 4)]
        return remote(source, target, self.x_send.at[index], self.x_recv.at[index], here.at_x(step))

    def start(self):
        for index in range(4):
            self.x_copy(index).start()

    def combine(self):
        for way in range(2):
            self.x_copy(way).wait_recv()
            owner = (self.here.x + 1 - 2 * way) % NX
            self.terms[pl.ds(4 * way, 4), owner] = self.terms[pl.ds(4 * way, 4), owner] + self.early[way]
            self.x_copy(4 + way).start()

    def y_copy(self, step):
        return remote(
            self.kept.at[place_of((self.here.y + step) % NY)], self.arrivals.at[step],
            self.y_send.at[step], self.y_recv.at[step], self.here.at_y(step),
        )

    def along_y(self):
        for index in range(2, 6):
            self.x_copy(index).wait_recv()
        self.kept[...] = self.terms[:, self.here.x] + (self.late[0] + self.late[1])
        for step in (4, 3, 5, 2, 6, 1, 7):
            self.y_copy(step).start()

    def finish(self):
        value = self.kept[place_of(self.here.y)]
        for step in (1, 7, 2, 6, 3, 5, 4):
            self.y_copy(step).wait_recv()
            value = value + self.arrivals[step]
        return value

    def wait_send(self):
        for index in range(6):
            self.x_copy(index).wait_send()
        for step in range(1, NY):
            self.y_copy(step).wait_send()


LANES, GROUP, STEP = 128, 32, 8


def columns_of(block, begin, rows):
    return [jnp.broadcast_to(block[:, begin + l : begin + l + 1], (rows, LANES)) for l in range(STEP)]


def cholesky_panels(gram, upper, inverse, work):
    line = lax.broadcasted_iota(jnp.int32, (GROUP, LANES), 0)
    rows_all = lax.broadcasted_iota(jnp.int32, (NB, NB), 0)
    cols_all = lax.broadcasted_iota(jnp.int32, (NB, NB), 1)
    work[:, :NB] = gram
    work[:, NB:] = jnp.where(rows_all == cols_all, 1.0, 0.0)
    for base in range(0, NB, GROUP):
        first, last = base // LANES, 2 + base // LANES + 1
        blocks = {q: work[base : base + GROUP, LANES * q : LANES * (q + 1)] for q in range(first, last)}
        for sub in range(0, GROUP, STEP):
            count = GROUP - sub
            number = line[:count]
            cols = columns_of(blocks[first], (base + sub) % LANES, count)
            scale = jnp.ones((STEP, LANES), jnp.float32)
            for j in range(STEP):
                pivot = cols[j][j : j + 1]
                over = 1.0 / pivot
                scale = jnp.where(number[:STEP] == j, lax.rsqrt(pivot), scale)
                factor = jnp.where(number > j, cols[j] * over, 0.0)
                for l in range(j + 1, STEP):
                    cols[l] = cols[l] - factor * cols[l][j : j + 1]
                for q in blocks:
                    blocks[q] = blocks[q] - factor * blocks[q][j : j + 1]
            for q in blocks:
                work[base + sub : base + sub + STEP, LANES * q : LANES * (q + 1)] = blocks[q][:STEP] * scale
                blocks[q] = blocks[q][STEP:]
        after = base + GROUP
        if after < NB:
            start = after // LANES
            left = work[base:after, LANES * start : NB]
            right = work[base:after, LANES * start : LANES * last]
            change = dot(left, right, ((0,), (0,)))
            work[after:, LANES * start : LANES * last] -= change[after - LANES * start :]
        else:
            upper[...] = jnp.where(rows_all <= cols_all, work[:, :NB], 0.0)
            inverse[...] = work[:, NB:]
        yield base // GROUP


def inverse_panels(square, pad):
    lane = lax.broadcasted_iota(jnp.int32, (GROUP, LANES), 1)
    line = lax.broadcasted_iota(jnp.int32, (GROUP, LANES), 0)
    pad[...] = jnp.zeros_like(pad)
    lane_all = lax.broadcasted_iota(jnp.int32, (NB, LANES), 1)
    for base in range(0, NB, GROUP):
        home, offset = base // LANES, base % LANES
        blocks = {q: square[base : base + GROUP, LANES * q : LANES * (q + 1)] for q in range(2)}
        blocks[2] = jnp.where(lane == line + offset, 1.0, 0.0)
        scale = jnp.ones((GROUP, LANES), jnp.float32)
        for sub in range(0, GROUP, STEP):
            cols = columns_of(blocks[home], offset + sub, GROUP)
            for j in range(STEP):
                row = sub + j
                over = 1.0 / cols[j][row : row + 1]
                scale = jnp.where(line == row, over, scale)
                factor = jnp.where(line == row, 0.0, cols[j] * over)
                for l in range(j + 1, STEP):
                    cols[l] = cols[l] - factor * cols[l][row : row + 1]
                for q in blocks:
                    blocks[q] = blocks[q] - factor * blocks[q][row : row + 1]
        inside = jnp.logical_and(lane >= offset, lane < offset + GROUP)
        blocks = {q: blocks[q] * scale for q in blocks}
        blocks[home] = jnp.where(inside, blocks[2], blocks[home])
        for q in range(2):
            pad[offset : offset + GROUP, LANES * q : LANES * (q + 1)] = blocks[q]
        mine = square[:, LANES * home : LANES * (home + 1)]
        inside_all = jnp.logical_and(lane_all >= offset, lane_all < offset + GROUP)
        change = dot(jnp.where(inside_all, mine, 0.0), pad[...])
        square[:, LANES * home : LANES * (home + 1)] = jnp.where(inside_all, 0.0, mine)
        square[...] -= change
        square[base : base + GROUP, :] = pad[offset : offset + GROUP, :]
        pad[offset : offset + GROUP, :] = jnp.zeros((GROUP, NB), jnp.float32)
        yield base // GROUP


def ones_at(shape, begin, here_too):
    rows = lax.broadcasted_iota(jnp.int32, shape, 0) + begin
    cols = lax.broadcasted_iota(jnp.int32, shape, 1)
    return jnp.where(jnp.logical_and(rows == cols, here_too), 1.0, 0.0)


def vmem(*shape):
    return jax.ShapeDtypeStruct(shape, jnp.float32)


def scratch(*shape):
    return pltpu.VMEM(shape, jnp.float32)


def dma(n):
    return pltpu.SemaphoreType.DMA((n,))


OUTS = {
    "update": (2 * NB, NB), "vectors": (2 * NB, NB), "vectors_cols": (4 * NB, NB),
    "scaled_cols": (8, 4, SLICE, NB), "upper": (NB, NB),
}
BUFFERS = {
    "whole": (PIECE, PIECE, 2 * NB), "slab": (2 * NB, NB), "own": (SLICE, NB),
    "gram_x": (NX, PIECE, NB), "gram_y": (NY, PIECE, NB), "gram": (PIECE, PIECE, NB), "top": (PIECE, PIECE, NB),
    "columns": (8, 4, SLICE, NB), "pair": (2 * SLICE, NB), "corner": (SLICE, NB), "corner_here": (SLICE, NB),
    "terms": (8, 4, SLICE, NB), "early": (2, 4, SLICE, NB), "late": (2, 8, SLICE, NB),
    "kept": (8, SLICE, NB), "arrivals": (NY, SLICE, NB),
    "work": (NB, 2 * NB), "inverse": (NB, NB), "transform": (NB, NB), "pad": (LANES, NB),
    "inner": (NZ, 2, PIECE, NB), "inner_other": (NZ, PIECE, NB), "inner_arrivals": (NZ, PIECE, NB),
    "sum_x": (NX, PIECE, NB), "sum_y": (NY, PIECE, NB), "coupling": (PIECE, PIECE, NB),
    "scaled_own": (SLICE, NB), "scaled": (PIECE, SLICE, NB),
}
LINE = [NZ] * 4
TOTAL = [NX, NX, NY, NY] + LINE
SPREAD = [NY, NY, 6, 6]
SEMS = {
    "line": LINE, "gram": TOTAL, "tops": LINE, "top": [NX + NY, 2], "corner": [NZ + 1, 2],
    "swap_panel": [2], "swap_corner": [2], "swap_scaled": [2], "columns": SPREAD, "plane": [6, 6, NY, NY],
    "core": [2], "inner": [NZ, NZ], "coupling": TOTAL, "scaled_cols": SPREAD, "scaled": LINE,
}


def panel_kernel(piece, square, *refs):
    names = list(OUTS) + list(BUFFERS)
    b = dict(zip(names, refs))
    sems, rest = {}, list(refs[len(names) :])
    for name, counts in SEMS.items():
        sems[name], rest = rest[: len(counts)], rest[len(counts) :]

    here = Place()
    line = Line(here, lambda c: b["whole"].at[c], *sems["line"])
    total = Total(here, b["gram_x"], b["gram_y"], b["gram"], sems["gram"])
    tops = Line(here, lambda c: b["top"].at[c], *sems["tops"])
    columns = Spread(here, b["columns"], *sems["columns"])
    plane = PlaneSum(
        here, b["terms"], b["early"], b["late"], b["kept"], b["arrivals"], *sems["plane"]
    )
    coupling = Total(here, b["sum_x"], b["sum_y"], b["coupling"], sems["coupling"])
    scaled_cols = Spread(here, b["scaled_cols"], *sems["scaled_cols"])
    scaled_line = Line(here, lambda c: b["scaled"].at[c], *sems["scaled"])
    place = lambda row: (place_of(row // NX), row % NX)
    swap_panel = Swap(
        here, b["own"], lambda row, col: b["columns"].at[place(row)], sems["swap_panel"][0]
    )
    swap_corner = Swap(
        here, b["corner"], lambda row, col: b["corner_here"], sems["swap_corner"][0]
    )
    swap_scaled = Swap(
        here, b["scaled_own"], lambda row, col: b["scaled"].at[col], sems["swap_scaled"][0]
    )
    here.greet()

    b["whole"][here.col] = piece[...]
    line.start()
    corner_send, corner_recv = sems["corner"]

    def corner_copy(z, index):
        return remote(
            square.at[pl.ds(2 * SLICE * z, 2 * SLICE), pl.ds(0, NB)], b["pair"],
            corner_send.at[index], corner_recv.at[0], (here.row, 2 * z),
        )

    def corner_hand():
        return remote(
            b["pair"].at[pl.ds(SLICE, SLICE), :], b["corner"],
            corner_send.at[NZ], corner_recv.at[1], here.sibling,
        )

    @pl.when(here.col == 0)
    def _():
        for z in range(1, NZ):
            corner_copy(z, z).start()
        b["pair"][...] = square[pl.ds(0, 2 * SLICE), pl.ds(0, NB)]

    line.finish()
    slab = b["slab"]
    slab[...] = b["whole"][...].reshape(NB, 2 * NB).T
    b["own"][...] = slab[pl.ds(pl.multiple_of(SLICE * here.col, SLICE), SLICE), :]
    swap_panel.start()
    total.along_x(dot(piece[...], slab[...]))

    top_send, top_recv = sems["top"]

    def top_x(step):
        ref = b["top"].at[here.col]
        return remote(ref, ref, top_send.at[step], top_recv.at[0], here.at_x(step))

    def top_y(step):
        ref = b["top"].at[here.col]
        return remote(ref, ref, top_send.at[NX + step], top_recv.at[1], here.at_y(step))

    @pl.when(here.row == 0)
    def _():
        b["top"][here.col] = slab[pl.ds(pl.multiple_of(PIECE * here.col, PIECE), PIECE), :]
        for step in range(1, NX):
            top_x(step).start()

    product = dot(square[...], slab[...], ((0,), (0,)))
    b["terms"][...] = product.reshape(8, 4, SLICE, NB)
    plane.start()
    total.along_y()

    @pl.when(here.y == 0)
    def _():
        @pl.when(here.x > 0)
        def _():
            top_x(1).wait_recv()

        for step in range(1, NY):
            top_y(step).start()

    @pl.when(here.core == 0)
    def _():
        @pl.when(here.z > 0)
        def _():
            corner_copy(here.z, 0).wait_recv()

        corner_hand().start()
        b["corner"][...] = b["pair"][pl.ds(0, SLICE), :]

    @pl.when(here.core == 1)
    def _():
        corner_hand().wait_recv()

    swap_corner.start()
    plane.combine()

    @pl.when(here.y > 0)
    def _():
        top_y(1).wait_recv()

    total.along_z()
    tops.start()
    plane.along_y()
    swap_panel.wait_recv()
    total.finish()
    tops.finish()

    share = None
    for step in cholesky_panels(b["gram"][...].reshape(NB, NB), b["upper"], b["inverse"], b["work"]):
        if step == 1:
            share = plane.finish()
            columns.along_y()
    swap_corner.wait_recv()
    inverse = b["inverse"]
    product = dot(share, inverse[...], ((1,), (1,))) + b["corner_here"][...]
    mine = b["columns"][place(here.row)]
    vectors_here = dot(mine, inverse[...], ((1,), (1,)))
    vectors_here = vectors_here + ones_at(
        (SLICE, NB), SLICE * here.row, jnp.logical_and(here.col == 0, here.row < NB // SLICE)
    )
    b["inner"][...] = dot(vectors_here, product, ((0,), (0,))).reshape(NZ, 2, PIECE, NB)
    core = remote(
        b["inner"].at[:, 1 - here.core], b["inner_other"], sems["core"][0].at[0], sems["core"][0].at[1], here.sibling
    )
    core.start()
    inner_send, inner_recv = sems["inner"]

    def inner_copy(step):
        return remote(
            b["inner_other"].at[(here.z + step) % NZ], b["inner_arrivals"].at[step],
            inner_send.at[step], inner_recv.at[step], here.at_z(step),
        )

    transform = b["transform"]
    transform[...] = dot(inverse[...], b["top"][...].reshape(NB, NB), ((1,), (1,))) + ones_at(
        (NB, NB), 0, True
    )
    for step in inverse_panels(transform, b["pad"]):
        if step == 1:
            core.wait_recv()
            b["inner_other"][...] = b["inner_other"][...] + b["inner"][:, here.core]
            for hop in (4, 3, 5, 2, 6, 1, 7):
                inner_copy(hop).start()
        if step == 2:
            columns.along_x()
        if step == 5:
            value = b["inner_other"][here.z]
            for hop in (1, 7, 2, 6, 3, 5, 4):
                inner_copy(hop).wait_recv()
                value = value + b["inner_arrivals"][hop]
            coupling.along_x(value)
            columns.forward()
    scaled = dot(product, transform[...])
    b["scaled_own"][...] = scaled
    b["scaled_cols"][place(here.row)] = scaled
    swap_scaled.start()
    scaled_cols.along_y()
    coupling.along_y()
    b["vectors"][...] = dot(slab[...], inverse[...], ((1,), (1,))) + ones_at(
        (2 * NB, NB), 0, here.row == 0
    )
    swap_scaled.wait_recv()
    scaled_line.start()
    columns.finish()
    b["vectors_cols"][...] = dot(
        b["columns"][...].reshape(4 * NB, NB), inverse[...], ((1,), (1,))
    ) + ones_at((4 * NB, NB), 0, here.col == 0)
    coupling.along_z()
    scaled_cols.along_x()
    scaled_line.finish()
    coupling.finish()
    middle = dot(b["coupling"][...].reshape(NB, NB), transform[...])
    middle = dot(transform[...], middle, ((0,), (0,)))
    scaled_cols.forward()
    b["update"][...] = b["scaled"][...].reshape(2 * NB, NB) - dot(b["vectors"][...], middle)
    scaled_cols.finish()

    core.wait_send()
    for hop in range(1, NZ):
        inner_copy(hop).wait_send()

    @pl.when(here.col == 0)
    def _():
        for z in range(1, NZ):
            corner_copy(z, z).wait_send()

    @pl.when(here.core == 0)
    def _():
        corner_hand().wait_send()

    @pl.when(here.row == 0)
    def _():
        for step in range(1, NX):
            top_x(step).wait_send()

    @pl.when(here.y == 0)
    def _():
        for step in range(1, NY):
            top_y(step).wait_send()

    for sent in (
        line, total, tops, columns, plane, coupling, scaled_cols, scaled_line, swap_panel, swap_corner, swap_scaled
    ):
        sent.wait_send()


def per_device(panel, matrix):
    square = matrix.reshape(2 * NB, 4 * NB)
    piece = panel.reshape(2 * NB, PIECE).T
    whole = pl.BlockSpec(memory_space=pltpu.VMEM)
    update, vectors, vectors_cols, scaled_cols, upper = pl.pallas_call(
        panel_kernel,
        out_shape=[vmem(*shape) for shape in OUTS.values()],
        in_specs=[whole] * 2,
        out_specs=[whole] * len(OUTS),
        scratch_shapes=[scratch(*shape) for shape in BUFFERS.values()]
        + [dma(n) for counts in SEMS.values() for n in counts],
        compiler_params=pltpu.CompilerParams(
            collective_id=0, has_side_effects=True, vmem_limit_bytes=VMEM_LIMIT
        ),
        name="panel",
    )(piece, square)
    left = jnp.concatenate([update, vectors], axis=1)
    right = jnp.concatenate([vectors_cols, scaled_cols.reshape(4 * NB, NB)], axis=1)
    updated = square - dot(left, right, ((1,), (1,)))
    return (updated.reshape(matrix.shape), upper)


def solution(mesh):
    in_specs = (P(None, "row", "col"), P(None, "row", None, "col"))
    out_specs = (P(None, "row", None, "col"), P())
    return jax.shard_map(
        per_device, mesh=mesh, in_specs=in_specs, out_specs=out_specs, check_vma=False
    )
```

time: 288 us -> 107 us (0.37); the launches traced: 284 us -> 107 us
  other arithmetic: 115 us -> 0 us
  Pallas kernels: 120 us -> 97 us
  local copies, waits for them, and re-layouts: 27.5 us -> 5.51 us
  matrix products: 17.6 us -> 3.57 us
  between operations: 3.76 us -> 0.65 us
    another operation x19 -> x0, other arithmetic: 111 us -> none  [the longest x6 35.5 us: per_device(): lower_one = jnp.linalg.cholesky(gram.reshape(NB, NB))]
    pallas_call x2 -> x1, Pallas kernels: 120 us -> 97 us  [per_device(): pl.pallas_call(panel_kernel, out_shape=[vmem(*shape) for shape in OUTS.va...]
    another operation x20 -> x0, local copies, waits for them, and re-layouts: 9.98 us -> none  [the longest x9 6.02 us: per_device(): lax.linalg.triangular_solve(lower_one, identity, left_side=True, lower=True)]
    another operation x13 -> x0, matrix products: 8.73 us -> none  [the longest x3 3.61 us: per_device(): lax.linalg.triangular_solve(lower_one, identity, left_side=True, lower=True)]
    unnamed x23 -> x2, local copies, waits for them, and re-layouts: 10.4 us -> 2.76 us
    dot_general x2 -> x1, matrix products: 7.83 us -> 3.57 us  [dot(): lax.dot_general(left, right, (contract, ((), ())), preferred_element_type...]
    reshape x3 -> x1, local copies, waits for them, and re-layouts: 5.29 us -> 1.99 us  [per_device(): return (updated.reshape(matrix.shape), upper)]
where the time goes in v3:
time: 107 us
  Pallas kernels  97 us (91%)
  local copies, waits for them, and re-layouts  5.51 us (5%)
  matrix products  3.57 us (3%)
    pallas_call x1, Pallas kernels, per_device(): pl.pallas_call(panel_kernel, out_shape=[vmem(*shape) for shape in OUTS.va...  97 us
    dot_general x1, matrix products, dot(): lax.dot_general(left, right, (contract, ((), ())), preferred_element_type...  3.57 us
    unnamed x2, local copies, waits for them, and re-layouts  2.76 us

profile of v3, /device:TPU:1, one launch (start us, length us, event | category | flops | bytes accessed | tf_op | source)
XLA Modules:
  0.0 106.7 jit_solution(6914971478199029090)
XLA Ops:
  0.6 0.8 copy.5
  1.4 2.1 %copy.6 = f32[64,8,4,256]{3,1,2,0:T(8,128)S(1)} copy(f32[64,8,4,256]{3,2,1,0:T(4,128)} %bitcast.12) | data formatting | bytes 4194304
  3.5 97.0 %panel.1 = (f32[512,256]{1,0:T(8,128)S(1)}, f32[512,256]{1,0:T(8,128)S(1)}, f32[1024,256]{1,0:T(8,128)S(1)}, f32[8,4,32,256]{3,2,1,0:T(8,128)S(1)}, f32[256,256]{1,0:T(8,128)S(1)}) custom-call(f32[16,512]{1,0:T(8,128)S(1)} %bitcast.11, f32[512,1024]{1,0:T(8,128)S(1)} %bitcast.8), custom_call_target="tpu_custom_call" | custom-call | tf_op jit(solution)/shard_map/panel/pallas_call | solution.py:630
  100.4 3.6 %fusion.4 = f32[512,1024]{1,0:T(8,128)S(1)} fusion(f32[512,1024]{1,0:T(8,128)S(1)} %bitcast.9, f32[1024,256]{1,0:T(8,128)S(1)} %bitcast.10, f32[1024,256]{1,0:T(8,128)S(1)} %get-tuple-element.9, f32[512,256]{1,0:T(8,128)S(1)} %get-tuple-element.8, f32[512,256]{1,0:T(8,128)S(1)} %get-tuple-element.7), kind=kOutput, calls=%fused_computation.4 | convolution fusion | flops 3222536192 | bytes 7340032 | tf_op jit(solution)/shard_map/dot_general | solution.py:20
  104.0 2.0 %reshape.19 = f32[2,256,4,256]{3,2,1,0:T(4,128)} reshape(f32[512,1024]{1,0:T(8,128)S(1)} %fusion.4) | data formatting | bytes 4194304 | tf_op jit(solution)/shard_map/reshape | solution.py:645
  106.0 0.7 copy.8

commit v4 on v3

--- a/solution.py
+++ b/solution.py
@@ -1,4 +1,4 @@
-import functools
+import types
 
 import jax
 import jax.numpy as jnp
@@ -13,6 +13,7 @@
 NB = 256
 PIECE = 16
 SLICE = 32
+ROWS = 128
 VMEM_LIMIT = 40 * 1024 * 1024
 
 
@@ -383,74 +384,80 @@
     return pltpu.SemaphoreType.DMA((n,))
 
 
-OUTS = {
-    "update": (2 * NB, NB), "vectors": (2 * NB, NB), "vectors_cols": (4 * NB, NB),
-    "scaled_cols": (8, 4, SLICE, NB), "upper": (NB, NB),
-}
-BUFFERS = {
-    "whole": (PIECE, PIECE, 2 * NB), "slab": (2 * NB, NB), "own": (SLICE, NB),
-    "gram_x": (NX, PIECE, NB), "gram_y": (NY, PIECE, NB), "gram": (PIECE, PIECE, NB), "top": (PIECE, PIECE, NB),
-    "columns": (8, 4, SLICE, NB), "pair": (2 * SLICE, NB), "corner": (SLICE, NB), "corner_here": (SLICE, NB),
-    "terms": (8, 4, SLICE, NB), "early": (2, 4, SLICE, NB), "late": (2, 8, SLICE, NB),
-    "kept": (8, SLICE, NB), "arrivals": (NY, SLICE, NB),
-    "work": (NB, 2 * NB), "inverse": (NB, NB), "transform": (NB, NB), "pad": (LANES, NB),
-    "inner": (NZ, 2, PIECE, NB), "inner_other": (NZ, PIECE, NB), "inner_arrivals": (NZ, PIECE, NB),
-    "sum_x": (NX, PIECE, NB), "sum_y": (NY, PIECE, NB), "coupling": (PIECE, PIECE, NB),
-    "scaled_own": (SLICE, NB), "scaled": (PIECE, SLICE, NB),
-}
+OUTS = dict(
+    update=(2 * NB, NB), turned=(2 * NB, NB), vectors_cols=(4 * NB, NB),
+    product_cols=(8, 4, SLICE, NB), upper=(NB, NB),
+)
+BUFFERS = dict(
+    square=(2 * NB, 4 * NB), whole=(PIECE, PIECE, 2 * NB), slab=(2 * NB, NB), own=(SLICE, NB),
+    gram_x=(NX, PIECE, NB), gram_y=(NY, PIECE, NB), gram=(PIECE, PIECE, NB), top=(PIECE, PIECE, NB),
+    columns=(8, 4, SLICE, NB), pair=(2 * SLICE, NB), corner=(SLICE, NB), corner_here=(SLICE, NB),
+    terms=(8, 4, SLICE, NB), early=(2, 4, SLICE, NB), late=(2, 8, SLICE, NB),
+    kept=(8, SLICE, NB), arrivals=(NY, SLICE, NB),
+    work=(NB, 2 * NB), inverse=(NB, NB), transform=(NB, NB), pad=(LANES, NB),
+    inner=(NZ, 2, PIECE, NB), inner_other=(NZ, PIECE, NB), inner_arrivals=(NZ, PIECE, NB),
+    sum_x=(NX, PIECE, NB), sum_y=(NY, PIECE, NB), coupling=(PIECE, PIECE, NB),
+    share=(SLICE, NB), product_own=(SLICE, NB), product=(PIECE, SLICE, NB), vectors=(2 * NB, NB),
+    crown_own=(2, 2, PIECE, NB), crown_pair=(2, 2, PIECE, NB), crown=(PIECE, 2, PIECE, NB),
+)
 LINE = [NZ] * 4
 TOTAL = [NX, NX, NY, NY] + LINE
 SPREAD = [NY, NY, 6, 6]
-SEMS = {
-    "line": LINE, "gram": TOTAL, "tops": LINE, "top": [NX + NY, 2], "corner": [NZ + 1, 2],
-    "swap_panel": [2], "swap_corner": [2], "swap_scaled": [2], "columns": SPREAD, "plane": [6, 6, NY, NY],
-    "core": [2], "inner": [NZ, NZ], "coupling": TOTAL, "scaled_cols": SPREAD, "scaled": LINE,
-}
-
-
-def panel_kernel(piece, square, *refs):
+SEMS = dict(
+    line=LINE, gram=TOTAL, tops=LINE, top=[NX + NY, 2], corner=[NZ + 1, 2],
+    swap_panel=[2], swap_corner=[2], swap_product=[2], columns=SPREAD, plane=[6, 6, NY, NY],
+    core=[2], inner=[NZ, NZ], coupling=TOTAL, product_cols=SPREAD, product=LINE,
+    crown_in=[2, 2], crown_out=[NX + NY, 2], crown=LINE,
+)
+
+
+def panel_kernel(piece, matrix, *refs):
     names = list(OUTS) + list(BUFFERS)
-    b = dict(zip(names, refs))
-    sems, rest = {}, list(refs[len(names) :])
+    b = types.SimpleNamespace(**dict(zip(names, refs)))
+    sems, rest = types.SimpleNamespace(), list(refs[len(names) :])
     for name, counts in SEMS.items():
-        sems[name], rest = rest[: len(counts)], rest[len(counts) :]
+        setattr(sems, name, rest[: len(counts)])
+        rest = rest[len(counts) :]
 
     here = Place()
-    line = Line(here, lambda c: b["whole"].at[c], *sems["line"])
-    total = Total(here, b["gram_x"], b["gram_y"], b["gram"], sems["gram"])
-    tops = Line(here, lambda c: b["top"].at[c], *sems["tops"])
-    columns = Spread(here, b["columns"], *sems["columns"])
+    line = Line(here, lambda c: b.whole.at[c], *sems.line)
+    total = Total(here, b.gram_x, b.gram_y, b.gram, sems.gram)
+    tops = Line(here, lambda c: b.top.at[c], *sems.tops)
+    columns = Spread(here, b.columns, *sems.columns)
     plane = PlaneSum(
-        here, b["terms"], b["early"], b["late"], b["kept"], b["arrivals"], *sems["plane"]
-    )
-    coupling = Total(here, b["sum_x"], b["sum_y"], b["coupling"], sems["coupling"])
-    scaled_cols = Spread(here, b["scaled_cols"], *sems["scaled_cols"])
-    scaled_line = Line(here, lambda c: b["scaled"].at[c], *sems["scaled"])
+        here, b.terms, b.early, b.late, b.kept, b.arrivals, *sems.plane
+    )
+    coupling = Total(here, b.sum_x, b.sum_y, b.coupling, sems.coupling)
+    product_cols = Spread(here, b.product_cols, *sems.product_cols)
+    product_line = Line(here, lambda c: b.product.at[c], *sems.product)
+    crown_line = Line(here, lambda c: b.crown.at[c], *sems.crown)
     place = lambda row: (place_of(row // NX), row % NX)
     swap_panel = Swap(
-        here, b["own"], lambda row, col: b["columns"].at[place(row)], sems["swap_panel"][0]
+        here, b.own, lambda row, col: b.columns.at[place(row)], sems.swap_panel[0]
     )
     swap_corner = Swap(
-        here, b["corner"], lambda row, col: b["corner_here"], sems["swap_corner"][0]
-    )
-    swap_scaled = Swap(
-        here, b["scaled_own"], lambda row, col: b["scaled"].at[col], sems["swap_scaled"][0]
+        here, b.corner, lambda row, col: b.corner_here, sems.swap_corner[0]
+    )
+    swap_product = Swap(
+        here, b.product_own, lambda row, col: b.product.at[col], sems.swap_product[0]
     )
     here.greet()
 
-    b["whole"][here.col] = piece[...]
+    b.whole[here.col] = piece[...]
     line.start()
-    corner_send, corner_recv = sems["corner"]
+    square = b.square
+    square[:, :NB] = matrix[:, 0, :]
+    corner_send, corner_recv = sems.corner
 
     def corner_copy(z, index):
         return remote(
-            square.at[pl.ds(2 * SLICE * z, 2 * SLICE), pl.ds(0, NB)], b["pair"],
+            square.at[pl.ds(2 * SLICE * z, 2 * SLICE), pl.ds(0, NB)], b.pair,
             corner_send.at[index], corner_recv.at[0], (here.row, 2 * z),
         )
 
     def corner_hand():
         return remote(
-            b["pair"].at[pl.ds(SLICE, SLICE), :], b["corner"],
+            b.pair.at[pl.ds(SLICE, SLICE), :], b.corner,
             corner_send.at[NZ], corner_recv.at[1], here.sibling,
         )
 
@@ -458,34 +465,39 @@
     def _():
         for z in range(1, NZ):
             corner_copy(z, z).start()
-        b["pair"][...] = square[pl.ds(0, 2 * SLICE), pl.ds(0, NB)]
-
+        b.pair[...] = square[pl.ds(0, 2 * SLICE), pl.ds(0, NB)]
+
+    for d in range(1, 4):
+        square[:, NB * d : NB * (d + 1)] = matrix[:, d, :]
     line.finish()
-    slab = b["slab"]
-    slab[...] = b["whole"][...].reshape(NB, 2 * NB).T
-    b["own"][...] = slab[pl.ds(pl.multiple_of(SLICE * here.col, SLICE), SLICE), :]
-    swap_panel.start()
+    slab = b.slab
+    slab[...] = b.whole[...].reshape(NB, 2 * NB).T
     total.along_x(dot(piece[...], slab[...]))
 
-    top_send, top_recv = sems["top"]
+    top_send, top_recv = sems.top
 
     def top_x(step):
-        ref = b["top"].at[here.col]
+        ref = b.top.at[here.col]
         return remote(ref, ref, top_send.at[step], top_recv.at[0], here.at_x(step))
 
     def top_y(step):
-        ref = b["top"].at[here.col]
+        ref = b.top.at[here.col]
         return remote(ref, ref, top_send.at[NX + step], top_recv.at[1], here.at_y(step))
 
     @pl.when(here.row == 0)
     def _():
-        b["top"][here.col] = slab[pl.ds(pl.multiple_of(PIECE * here.col, PIECE), PIECE), :]
+        b.top[here.col] = slab[pl.ds(pl.multiple_of(PIECE * here.col, PIECE), PIECE), :]
         for step in range(1, NX):
             top_x(step).start()
 
-    product = dot(square[...], slab[...], ((0,), (0,)))
-    b["terms"][...] = product.reshape(8, 4, SLICE, NB)
-    plane.start()
+    b.own[...] = slab[pl.ds(pl.multiple_of(SLICE * here.col, SLICE), SLICE), :]
+    swap_panel.start()
+
+    def term(half):
+        value = dot(square[:, 2 * NB * half : 2 * NB * (half + 1)], slab[...], ((0,), (0,)))
+        b.terms[4 * half : 4 * half + 4] = value.reshape(4, 4, SLICE, NB)
+
+    term(0)
     total.along_y()
 
     @pl.when(here.y == 0)
@@ -497,6 +509,9 @@
         for step in range(1, NY):
             top_y(step).start()
 
+    term(1)
+    plane.start()
+
     @pl.when(here.core == 0)
     def _():
         @pl.when(here.z > 0)
@@ -504,95 +519,180 @@
             corner_copy(here.z, 0).wait_recv()
 
         corner_hand().start()
-        b["corner"][...] = b["pair"][pl.ds(0, SLICE), :]
+        b.corner[...] = b.pair[pl.ds(0, SLICE), :]
 
     @pl.when(here.core == 1)
     def _():
         corner_hand().wait_recv()
 
     swap_corner.start()
+
+    @pl.when(here.y > 0)
+    def _():
+        top_y(1).wait_recv()
+
+    tops.start()
+    total.along_z()
     plane.combine()
-
-    @pl.when(here.y > 0)
-    def _():
-        top_y(1).wait_recv()
-
-    total.along_z()
-    tops.start()
+    swap_panel.wait_recv()
     plane.along_y()
-    swap_panel.wait_recv()
     total.finish()
     tops.finish()
 
-    share = None
-    for step in cholesky_panels(b["gram"][...].reshape(NB, NB), b["upper"], b["inverse"], b["work"]):
-        if step == 1:
-            share = plane.finish()
-            columns.along_y()
-    swap_corner.wait_recv()
-    inverse = b["inverse"]
-    product = dot(share, inverse[...], ((1,), (1,))) + b["corner_here"][...]
-    mine = b["columns"][place(here.row)]
-    vectors_here = dot(mine, inverse[...], ((1,), (1,)))
-    vectors_here = vectors_here + ones_at(
-        (SLICE, NB), SLICE * here.row, jnp.logical_and(here.col == 0, here.row < NB // SLICE)
-    )
-    b["inner"][...] = dot(vectors_here, product, ((0,), (0,))).reshape(NZ, 2, PIECE, NB)
+    crown_in_send, crown_in_recv = sems.crown_in
+    crown_send, crown_recv = sems.crown_out
+    source = here.row == here.z
+    level = here.y == here.z // NX
+
+    def crown_move():
+        return remote(
+            b.crown_own, b.crown_pair, crown_in_send.at[0], crown_in_recv.at[0], (here.row, 2 * here.row)
+        )
+
+    def crown_hand():
+        return remote(
+            b.crown_pair.at[:, 1], b.crown.at[2 * here.z + 1],
+            crown_in_send.at[1], crown_in_recv.at[1], here.sibling,
+        )
+
+    def crown_x(step):
+        ref = b.crown.at[here.col]
+        return remote(ref, ref, crown_send.at[step], crown_recv.at[0], here.at_x(step))
+
+    def crown_y(step):
+        ref = b.crown.at[here.col]
+        return remote(ref, ref, crown_send.at[NX + step], crown_recv.at[1], here.at_y(step))
+
+    def crown_first():
+        @pl.when(jnp.logical_and(here.col == 0, here.row < NZ))
+        def _():
+            b.crown_own[0] = b.share[...].reshape(2, PIECE, NB)
+            b.crown_own[1] = b.corner_here[...].reshape(2, PIECE, NB)
+
+            @pl.when(here.row > 0)
+            def _():
+                crown_move().start()
+
+            @pl.when(here.row == 0)
+            def _():
+                b.crown_pair[...] = b.crown_own[...]
+
+    def crown_second():
+        @pl.when(jnp.logical_and(source, here.core == 0))
+        def _():
+            @pl.when(here.z > 0)
+            def _():
+                crown_move().wait_recv()
+
+            crown_hand().start()
+            b.crown[here.col] = b.crown_pair[:, 0]
+
+    def crown_third():
+        @pl.when(source)
+        def _():
+            @pl.when(here.core == 1)
+            def _():
+                crown_hand().wait_recv()
+
+            for step in range(1, NX):
+                crown_x(step).start()
+
+    def crown_fourth():
+        @pl.when(level)
+        def _():
+            @pl.when(jnp.logical_not(source))
+            def _():
+                crown_x(1).wait_recv()
+
+            for step in range(1, NY):
+                crown_y(step).start()
+
+    def crown_fifth():
+        @pl.when(jnp.logical_not(level))
+        def _():
+            crown_y(1).wait_recv()
+
+        crown_line.start()
+
     core = remote(
-        b["inner"].at[:, 1 - here.core], b["inner_other"], sems["core"][0].at[0], sems["core"][0].at[1], here.sibling
-    )
-    core.start()
-    inner_send, inner_recv = sems["inner"]
+        b.inner.at[:, 1 - here.core], b.inner_other, sems.core[0].at[0], sems.core[0].at[1], here.sibling
+    )
+    inner_send, inner_recv = sems.inner
 
     def inner_copy(step):
         return remote(
-            b["inner_other"].at[(here.z + step) % NZ], b["inner_arrivals"].at[step],
+            b.inner_other.at[(here.z + step) % NZ], b.inner_arrivals.at[step],
             inner_send.at[step], inner_recv.at[step], here.at_z(step),
         )
 
-    transform = b["transform"]
-    transform[...] = dot(inverse[...], b["top"][...].reshape(NB, NB), ((1,), (1,))) + ones_at(
-        (NB, NB), 0, True
-    )
-    for step in inverse_panels(transform, b["pad"]):
+    for step in cholesky_panels(b.gram[...].reshape(NB, NB), b.upper, b.inverse, b.work):
         if step == 1:
+            b.share[...] = plane.finish()
+            inner = dot(b.columns[place(here.row)], b.share[...], ((0,), (0,)))
+            b.inner[...] = inner.reshape(NZ, 2, PIECE, NB)
+            core.start()
+            swap_corner.wait_recv()
+            crown_first()
+            columns.along_y()
+        if step == 3:
             core.wait_recv()
-            b["inner_other"][...] = b["inner_other"][...] + b["inner"][:, here.core]
+            b.inner_other[...] = b.inner_other[...] + b.inner[:, here.core]
             for hop in (4, 3, 5, 2, 6, 1, 7):
                 inner_copy(hop).start()
+        if step == 4:
+            crown_second()
+        if step == 6:
+            crown_third()
+    inverse, transform = b.inverse, b.transform
+    own = dot(b.share[...], inverse[...], ((1,), (1,))) + b.corner_here[...]
+    b.product_own[...] = own
+    b.product_cols[place(here.row)] = own
+    product_cols.along_y()
+    swap_product.start()
+    transform[...] = dot(inverse[...], b.top[...].reshape(NB, NB), ((1,), (1,))) + ones_at(
+        (NB, NB), 0, True
+    )
+    value = b.inner_other[here.z]
+    for hop in (1, 7, 2, 6, 3, 5, 4):
+        inner_copy(hop).wait_recv()
+        value = value + b.inner_arrivals[hop]
+    coupling.along_x(value)
+    for step in inverse_panels(transform, b.pad):
+        if step == 0:
+            crown_fourth()
         if step == 2:
+            coupling.along_y()
+        if step == 3:
             columns.along_x()
-        if step == 5:
-            value = b["inner_other"][here.z]
-            for hop in (1, 7, 2, 6, 3, 5, 4):
-                inner_copy(hop).wait_recv()
-                value = value + b["inner_arrivals"][hop]
-            coupling.along_x(value)
+        if step == 4:
+            crown_fifth()
+            swap_product.wait_recv()
+            product_line.start()
+        if step == 6:
             columns.forward()
-    scaled = dot(product, transform[...])
-    b["scaled_own"][...] = scaled
-    b["scaled_cols"][place(here.row)] = scaled
-    swap_scaled.start()
-    scaled_cols.along_y()
-    coupling.along_y()
-    b["vectors"][...] = dot(slab[...], inverse[...], ((1,), (1,))) + ones_at(
+        if step == 7:
+            coupling.along_z()
+    product_cols.along_x()
+    b.vectors[...] = dot(slab[...], inverse[...], ((1,), (1,))) + ones_at(
         (2 * NB, NB), 0, here.row == 0
     )
-    swap_scaled.wait_recv()
-    scaled_line.start()
+    b.turned[...] = dot(b.vectors[...], transform[...], ((1,), (1,)))
     columns.finish()
-    b["vectors_cols"][...] = dot(
-        b["columns"][...].reshape(4 * NB, NB), inverse[...], ((1,), (1,))
+    b.vectors_cols[...] = dot(
+        b.columns[...].reshape(4 * NB, NB), inverse[...], ((1,), (1,))
     ) + ones_at((4 * NB, NB), 0, here.col == 0)
-    coupling.along_z()
-    scaled_cols.along_x()
-    scaled_line.finish()
+    product_cols.forward()
+    crown_line.finish()
+    product_line.finish()
+    scaled = dot(b.product[...].reshape(2 * NB, NB), transform[...])
+    edge = dot(b.crown[:, 0].reshape(NB, NB), inverse[...], ((1,), (1,)))
+    edge = edge + edge.T + b.crown[:, 1].reshape(NB, NB)
     coupling.finish()
-    middle = dot(b["coupling"][...].reshape(NB, NB), transform[...])
-    middle = dot(transform[...], middle, ((0,), (0,)))
-    scaled_cols.forward()
-    b["update"][...] = b["scaled"][...].reshape(2 * NB, NB) - dot(b["vectors"][...], middle)
-    scaled_cols.finish()
+    middle = dot(inverse[...], b.coupling[...].reshape(NB, NB))
+    middle = dot(middle, inverse[...], ((1,), (1,))) + edge
+    middle = dot(transform[...], dot(middle, transform[...]), ((0,), (0,)))
+    b.update[...] = scaled - dot(b.vectors[...], middle)
+    product_cols.finish()
 
     core.wait_send()
     for hop in range(1, NZ):
@@ -617,17 +717,59 @@
         for step in range(1, NY):
             top_y(step).wait_send()
 
+    @pl.when(jnp.logical_and(here.col == 0, jnp.logical_and(here.row > 0, here.row < NZ)))
+    def _():
+        crown_move().wait_send()
+
+    @pl.when(source)
+    def _():
+        @pl.when(here.core == 0)
+        def _():
+            crown_hand().wait_send()
+
+        for step in range(1, NX):
+            crown_x(step).wait_send()
+
+    @pl.when(level)
+    def _():
+        for step in range(1, NY):
+            crown_y(step).wait_send()
+
     for sent in (
-        line, total, tops, columns, plane, coupling, scaled_cols, scaled_line, swap_panel, swap_corner, swap_scaled
+        line, total, tops, columns, plane, coupling, product_cols, product_line, crown_line,
+        swap_panel, swap_corner, swap_product,
     ):
         sent.wait_send()
 
 
+def split(value):
+    high = value.astype(jnp.bfloat16)
+    return high, (value - high.astype(jnp.float32)).astype(jnp.bfloat16)
+
+
+def update_kernel(update, turned, vectors_cols, product_cols, matrix, updated, high, low):
+    @pl.when(pl.program_id(0) == 0)
+    def _():
+        for k, ref in enumerate((vectors_cols, product_cols)):
+            high[k], low[k] = split(ref[...])
+
+    change = None
+    for k, ref in enumerate((update, turned)):
+        left_high, left_low = split(ref[...])
+        for left, right in ((left_high, low), (left_low, high), (left_high, high)):
+            term = lax.dot_general(
+                left, right[k], (((1,), (1,)), ((), ())), preferred_element_type=jnp.float32
+            )
+            change = term if change is None else change + term
+    for d in range(4):
+        updated[:, d, :] = matrix[:, d, :] - change[:, NB * d : NB * (d + 1)]
+
+
 def per_device(panel, matrix):
-    square = matrix.reshape(2 * NB, 4 * NB)
+    blocks = matrix.reshape(2 * NB, 4, NB)
     piece = panel.reshape(2 * NB, PIECE).T
     whole = pl.BlockSpec(memory_space=pltpu.VMEM)
-    update, vectors, vectors_cols, scaled_cols, upper = pl.pallas_call(
+    update, turned, vectors_cols, product_cols, upper = pl.pallas_call(
         panel_kernel,
         out_shape=[vmem(*shape) for shape in OUTS.values()],
         in_specs=[whole] * 2,
@@ -638,10 +780,20 @@
             collective_id=0, has_side_effects=True, vmem_limit_bytes=VMEM_LIMIT
         ),
         name="panel",
-    )(piece, square)
-    left = jnp.concatenate([update, vectors], axis=1)
-    right = jnp.concatenate([vectors_cols, scaled_cols.reshape(4 * NB, NB)], axis=1)
-    updated = square - dot(left, right, ((1,), (1,)))
+    )(piece, blocks)
+    rows = pl.BlockSpec((ROWS, NB), lambda i: (i, 0))
+    cols = pl.BlockSpec((4 * NB, NB), lambda i: (0, 0))
+    tile = pl.BlockSpec((ROWS, 4, NB), lambda i: (i, 0, 0))
+    updated = pl.pallas_call(
+        update_kernel,
+        grid=(2 * NB // ROWS,),
+        out_shape=vmem(2 * NB, 4, NB),
+        in_specs=[rows, rows, cols, cols, tile],
+        out_specs=tile,
+        scratch_shapes=[pltpu.VMEM((2, 4 * NB, NB), jnp.bfloat16) for _ in range(2)],
+        compiler_params=pltpu.CompilerParams(vmem_limit_bytes=VMEM_LIMIT),
+        name="update",
+    )(update, turned, vectors_cols, product_cols.reshape(4 * NB, NB), blocks)
     return (updated.reshape(matrix.shape), upper)
 
 

time: 107 us -> 103 us (0.963)
  matrix products: 3.57 us -> 0 us
  local copies, waits for them, and re-layouts: 5.51 us -> 3.06 us
  Pallas kernels: 97 us -> 99.2 us
    pallas_call x0 -> x1, Pallas kernels: none -> 6.48 us  [per_device(): pl.pallas_call(update_kernel, grid=(2 * NB // ROWS,), out_shape=vmem(2 *...]
    pallas_call x1, Pallas kernels: 97 us -> 92.7 us  [per_device(): pl.pallas_call(panel_kernel, out_shape=[vmem(*shape) for shape in OUTS.va...]
    dot_general x1 -> x0, matrix products: 3.57 us -> none  [dot(): lax.dot_general(left, right, (contract, ((), ())), preferred_element_type...]
    reshape x1 -> x0, local copies, waits for them, and re-layouts: 1.99 us -> none  [per_device(): return (updated.reshape(matrix.shape), upper)]
    unnamed x2 -> x5, local copies, waits for them, and re-layouts: 2.76 us -> 2.3 us
where the time goes in v4:
time: 103 us
  Pallas kernels  99.2 us (96%)
  local copies, waits for them, and re-layouts  3.06 us (3%)
    pallas_call x1, Pallas kernels, per_device(): pl.pallas_call(panel_kernel, out_shape=[vmem(*shape) for shape in OUTS.va...  92.7 us
    pallas_call x1, Pallas kernels, per_device(): pl.pallas_call(update_kernel, grid=(2 * NB // ROWS,), out_shape=vmem(2 *...  6.48 us
    unnamed x5, local copies, waits for them, and re-layouts  2.3 us

profile of v4, /device:TPU:1, one launch (start us, length us, event | category | flops | bytes accessed | tf_op | source)
XLA Modules:
  0.0 102.9 jit_solution(1163267390647648910)
XLA Ops:
  0.6 0.8 copy.5
  1.4 0.0 copy-start
  1.4 1.6 %copy-done = f32[2,256,4,256]{3,2,1,0:T(4,128)S(1)} copy-done((f32[2,256,4,256]{3,2,1,0:T(4,128)S(1)}, f32[2,256,4,256]{3,2,1,0:T(4,128)}, u32[]{:S(2)}) %copy-start) | copy-done | bytes 2097176
  3.0 0.0 copy-start.1
  3.0 92.7 %panel.1 = (f32[512,256]{1,0:T(8,128)S(1)}, f32[512,256]{1,0:T(8,128)S(1)}, f32[1024,256]{1,0:T(8,128)S(1)}, f32[8,4,32,256]{3,2,1,0:T(8,128)S(1)}, f32[256,256]{1,0:T(8,128)S(1)}) custom-call(f32[16,512]{1,0:T(8,128)S(1)} %bitcast.10, f32[512,4,256]{2,1,0:T(4,128)S(1)} %bitcast.7), custom_call_target="tpu_custom_call" | custom-call | tf_op jit(solution)/shard_map/panel/pallas_call | solution.py:772
  95.7 0.0 copy-done.1
  95.7 6.5 %update.1 = f32[512,4,256]{2,1,0:T(4,128)} custom-call(f32[512,256]{1,0:T(8,128)S(1)} %get-tuple-element.7.update, f32[512,256]{1,0:T(8,128)S(1)} %get-tuple-element.8.turned, f32[1024,256]{1,0:T(8,128)S(1)} %get-tuple-element.9.vectors_cols, f32[1024,256]{1,0:T(8,128)S(1)} %bitcast.9, f32[512,4,256]{2,1,0:T(4,128)S(1)} %bitcast.8), custom_call_target="tpu_custom_call" | custom-call | tf_op jit(solution)/shard_map/update/pallas_call | solution.py:787
  102.2 0.7 copy.7
Async XLA Ops:
  1.4 1.6 %copy-start = (f32[2,256,4,256]{3,2,1,0:T(4,128)S(1)}, f32[2,256,4,256]{3,2,1,0:T(4,128)}, u32[]{:S(2)}) copy-start(f32[2,256,4,256]{3,2,1,0:T(4,128)} %param.3) | copy-start | bytes 6291460
  3.0 92.7 %copy-start.1 = (f32[2,256,4,256]{3,2,1,0:T(4,128)S(1)}, f32[2,256,4,256]{3,2,1,0:T(4,128)}, u32[]{:S(2)}) copy-start(f32[2,256,4,256]{3,2,1,0:T(4,128)} %param.3) | copy-start | bytes 6291460
